TPU v7x, 128 devices: a whole 4x4x4 slice. The times are simulated.
128 devices in a mesh: shot: 32 (over z, x, core), line: 4 (over y).
Axes of the slice: x: 4, y: 4, z: 4, core: 2. Of those that a mesh axis runs over, the one named last changes fastest.
Arguments:
- traces: bfloat16 [65536, 2048], P(('shot', 'line')), may hold values from -12 to 12
- targets: bfloat16 [65536, 2048], P(('shot', 'line')), may hold values from -64 to 64
- src_local: int32 [65536], P(('shot', 'line')), may hold values from 0 to 3
- rcv_term: int32 [65536], P(('shot', 'line')), may hold values from 0 to 16383, as said below
- cmp_term: int32 [65536], P(('shot', 'line')), may hold values from 0 to 32767, as said below
- rcv_home: int32 [16384], replicated, may hold values from 0 to 16383, as said below
- cmp_home: int32 [32768], replicated, may hold values from 0 to 32767, as said below
- counts: int32 [128], P(('shot', 'line')), may hold values from 128 to 512, as said below
- src_filters: float32 [512, 128], P(('shot', 'line')), may hold values from -1.75 to 1.75
- rcv_filters: float32 [16384, 128], P(('shot', 'line')), may hold values from -1.75 to 1.75
- cmp_filters: float32 [32768, 128], P(('shot', 'line')), may hold values from -1.75 to 1.75
Outputs:
- src_out: float32 [512, 128], P(('shot', 'line'))
- rcv_out: float32 [16384, 128], P(('shot', 'line'))
- cmp_out: float32 [32768, 128], P(('shot', 'line'))
Inputs may be any that keep to these rules, and one draw needn't show every extreme that they name: Receiver row rcv_home[rcv_term[t]] lies on device rcv_home[rcv_term[t]] // 128. Among the 512 trace slots of one device (live or not) at most 8 have receiver rows on any one device; in every draw some device holds the receiver rows of exactly 8 slots of every device. `cmp_term`: likewise for CMP rows with 256 rows a device: at most 8 slots of one device name CMP rows on any one device, and some device is named so by exactly 8 slots of every device. `rcv_home`: A permutation of 0 to 16383. `cmp_home`: A permutation of 0 to 32767. The first counts[d] slots of device d are live; some device is full.
All inputs are finite; a program needn't handle non-finite values.
Results may differ from a plain program's by a relative error of at most 0.0027.
Values sent between devices are 32-bit elements; how exact they have to be, the bound alone decides.
No kernel may reach another device: no remote copies, remote signals or barrier semaphores. Data moves between devices by JAX's collectives and lax.ppermute only.
A program may use at most 64 MiB of HBM per device.

v0:
```python
import jax
import jax.numpy as jnp
from jax import lax
from jax.sharding import PartitionSpec as P

TBLK = 32


step_size = 0.5
highest = lax.Precision.HIGHEST


def pick_rows(table_rows, slot_index):
    flat_index = slot_index.reshape(-1)
    onehot = (
        flat_index[:, None] == jnp.arange(table_rows.shape[0], dtype=jnp.int32)[None, :]
    ).astype(jnp.float32)
    picked = jnp.dot(onehot, table_rows, precision=highest, preferred_element_type=jnp.float32)
    return picked.reshape(slot_index.shape + (table_rows.shape[1],))


def add_rows(slot_index, values, term_count):
    onehot = (
        slot_index.reshape(-1)[None, :] == jnp.arange(term_count, dtype=jnp.int32)[:, None]
    ).astype(jnp.float32)
    return jnp.dot(
        onehot,
        values.reshape(onehot.shape[1], -1),
        precision=highest,
        preferred_element_type=jnp.float32,
    )


def send_slots(slot_rows, terms_dev, device_count, slot_cap):
    owner_dev = slot_rows // terms_dev
    place_row = slot_rows % terms_dev
    onehot = (owner_dev[:, None] == jnp.arange(device_count, dtype=jnp.int32)[None, :]).astype(
        jnp.int32
    )
    before = jnp.cumsum(onehot, axis=0) - onehot
    rank_rows = jnp.sum(before * onehot, axis=1)
    slot_index = owner_dev * slot_cap + rank_rows
    request = jnp.zeros((device_count * slot_cap,), jnp.int32).at[slot_index].set(place_row)
    return (slot_index, request.reshape(device_count, slot_cap))


def settle(filter_table, slot_index, grad_in, power_in):
    term_count = filter_table.shape[0]
    sum_rows = add_rows(slot_index, grad_in, term_count)
    energy = add_rows(slot_index, power_in, term_count)[:, 0]
    return filter_table - step_size * sum_rows / jnp.maximum(energy, 1.0)[:, None]


def diagonal_sums(cross_before, cross_now):
    row_count, tap_count = (cross_now.shape[0], cross_now.shape[1])
    joined = jnp.concatenate([cross_before, cross_now], axis=2).reshape(
        row_count, 2 * tap_count * tap_count
    )
    padded = jnp.concatenate([joined, jnp.zeros((row_count, tap_count), jnp.float32)], axis=1)
    skewed = padded.reshape(row_count, tap_count, 2 * tap_count + 1)
    column_sums = jnp.sum(skewed, axis=1)
    return column_sums[:, 1 : tap_count + 1][:, ::-1]


def body(
    traces,
    targets,
    src_local,
    rcv_term,
    cmp_term,
    rcv_home,
    cmp_home,
    counts,
    src_filters,
    rcv_filters,
    cmp_filters,
):
    trace_rows, samples = traces.shape
    tap_count = src_filters.shape[1]
    device_count = lax.axis_size(("shot", "line"))
    slot_cap = max(2, 2 * trace_rows // device_count)
    rcv_index, rcv_request = send_slots(
        rcv_home[rcv_term], rcv_filters.shape[0], device_count, slot_cap
    )
    cmp_index, cmp_request = send_slots(
        cmp_home[cmp_term], cmp_filters.shape[0], device_count, slot_cap
    )
    requests = jnp.stack([rcv_request, cmp_request])
    received = lax.all_to_all(requests, ("shot", "line"), split_axis=1, concat_axis=1, tiled=True)
    values = jnp.stack([pick_rows(rcv_filters, received[0]), pick_rows(cmp_filters, received[1])])
    fetched = lax.all_to_all(values, ("shot", "line"), split_axis=1, concat_axis=1, tiled=True)
    fetched_rows = fetched.reshape(2, device_count * slot_cap, tap_count)
    src_onehot = (
        src_local[:, None] == jnp.arange(src_filters.shape[0], dtype=jnp.int32)[None, :]
    ).astype(jnp.float32)
    src_part = jnp.dot(
        src_onehot, src_filters, precision=highest, preferred_element_type=jnp.float32
    )
    mixed_filters = (src_part + fetched_rows[0][rcv_index] + fetched_rows[1][cmp_index]).astype(
        jnp.bfloat16
    )
    live_mask = (jnp.arange(trace_rows, dtype=jnp.int32) < counts[0]).astype(jnp.float32)
    block_count = samples // tap_count
    tap_range = jnp.arange(tap_count, dtype=jnp.int32)
    lag_index = tap_range[:, None, None]
    row_tap = tap_range[None, :, None]
    col_tap = tap_range[None, None, :]
    shift_upper = (col_tap - row_tap == lag_index).astype(jnp.bfloat16)
    shift_lower = (col_tap - row_tap + tap_count == lag_index).astype(jnp.bfloat16)

    def one_block(turn_index, carry):
        grad_rows, powers = carry
        start_row = turn_index * TBLK
        trace_block = lax.dynamic_slice_in_dim(traces, start_row, TBLK, 0).reshape(
            TBLK, block_count, tap_count
        )
        filter_block = lax.dynamic_slice_in_dim(mixed_filters, start_row, TBLK, 0)
        upper = jnp.einsum(
            "rk,kji->rji", filter_block, shift_upper, preferred_element_type=jnp.float32
        ).astype(jnp.bfloat16)
        lower = jnp.einsum(
            "rk,kji->rji", filter_block, shift_lower, preferred_element_type=jnp.float32
        ).astype(jnp.bfloat16)
        current = jnp.einsum("rbj,rji->rbi", trace_block, upper, preferred_element_type=jnp.float32)
        carried = jnp.einsum("rbj,rji->rbi", trace_block, lower, preferred_element_type=jnp.float32)
        model_block = current + jnp.concatenate(
            [jnp.zeros((TBLK, 1, tap_count), jnp.float32), carried[:, :-1]], axis=1
        )
        target_block = lax.dynamic_slice_in_dim(targets, start_row, TBLK, 0).reshape(
            TBLK, block_count, tap_count
        )
        alive_rows = lax.dynamic_slice_in_dim(live_mask, start_row, TBLK, 0)
        misfit = (
            alive_rows[:, None, None] * (model_block - target_block.astype(jnp.float32))
        ).astype(jnp.bfloat16)
        later = jnp.concatenate(
            [misfit[:, 1:], jnp.zeros((TBLK, 1, tap_count), jnp.bfloat16)], axis=1
        )
        cross_now = jnp.einsum(
            "rbi,rbj->rij", misfit, trace_block, preferred_element_type=jnp.float32
        )
        cross_before = jnp.einsum(
            "rbi,rbj->rij", later, trace_block, preferred_element_type=jnp.float32
        )
        grad_block = diagonal_sums(cross_before, cross_now)
        energy = alive_rows * jnp.sum(jnp.square(trace_block.astype(jnp.float32)), axis=(1, 2))
        grad_rows = lax.dynamic_update_slice_in_dim(grad_rows, grad_block, start_row, 0)
        powers = lax.dynamic_update_slice_in_dim(powers, energy, start_row, 0)
        return (grad_rows, powers)

    turn_count = trace_rows // TBLK
    grad_rows, powers = lax.fori_loop(
        0,
        turn_count,
        one_block,
        (jnp.zeros((trace_rows, tap_count), jnp.float32), jnp.zeros((trace_rows,), jnp.float32)),
    )
    empty_grad = jnp.zeros((device_count * slot_cap, tap_count), jnp.float32)
    empty_power = jnp.zeros((device_count * slot_cap,), jnp.float32)
    send_grad = jnp.stack(
        [empty_grad.at[rcv_index].set(grad_rows), empty_grad.at[cmp_index].set(grad_rows)]
    )
    send_power = jnp.stack(
        [empty_power.at[rcv_index].set(powers), empty_power.at[cmp_index].set(powers)]
    )
    got_grad, got_power = (
        lax.all_to_all(
            send_grad.reshape(2, device_count, slot_cap, tap_count),
            ("shot", "line"),
            split_axis=1,
            concat_axis=1,
            tiled=True,
        ),
        lax.all_to_all(
            send_power.reshape(2, device_count, slot_cap),
            ("shot", "line"),
            split_axis=1,
            concat_axis=1,
            tiled=True,
        ),
    )
    src_out = settle(src_filters, src_local, grad_rows, powers)
    rcv_out = settle(rcv_filters, received[0], got_grad[0], got_power[0])
    cmp_out = settle(cmp_filters, received[1], got_grad[1], got_power[1])
    return (src_out, rcv_out, cmp_out)


def solution(mesh):
    return jax.shard_map(
        body,
        mesh=mesh,
        in_specs=(
            P(("shot", "line"), None),
            P(("shot", "line"), None),
            P(("shot", "line")),
            P(("shot", "line")),
            P(("shot", "line")),
            P(),
            P(),
            P(("shot", "line")),
            P(("shot", "line"), None),
            P(("shot", "line"), None),
            P(("shot", "line"), None),
        ),
        out_specs=(P(("shot", "line"), None), P(("shot", "line"), None), P(("shot", "line"), None)),
        check_vma=False,
    )
```

profile of v0, /device:TPU:1, one launch (start us, length us, event | category | flops | bytes accessed | tf_op | source)
XLA Modules:
  0.0 588.4 jit_solution(3765068687075613206)
XLA Ops:
  15.6 21.6 %all_to_all.20 = s32[2,128,8]{2,0,1:T(2,128)S(1)} all-to-all(s32[2,128,8]{2,0,1:T(2,128)S(1)} %copy.41), channel_id=1, replica_groups=mesh['shot'=32,'line'=4] {'shot','line'}, dimensions={1} | all-to-all | bytes 16384 | tf_op jit(solution)/shard_map/all_to_all | solution.py:89
  44.6 18.8 %all-to-all-done.1 = f32[2,128,8,128]{3,2,0,1:T(8,128)S(1)} async-done(((f32[2,128,8,128]{3,2,0,1:T(8,128)}), f32[2,128,8,128]{3,2,0,1:T(8,128)S(1)}, u32[]{:S(2)}, u32[]{:S(2)}) %all-to-all-start.1) | async-done | bytes 1048608 | tf_op jit(solution)/shard_map/all_to_all | solution.py:91
  66.0 472.7 %while.16 = (s32[]{:T(128)}, f32[512,128]{1,0:T(8,128)S(1)}, f32[512]{0:T(512)S(1)}, f32[512]{0:T(512)S(1)}, bf16[512,2048]{1,0:T(8,128)(2,1)}, /*index=5*/bf16[...) while((s32[]{:T(128)}, f32[512,128]{1,0:T(8,128)S(1)}, ...), condition=%wide.region_11.12_spmd.clone, body=%wide.region_8.11_spmd.clone.sunk | while | flops 346550240 | bytes 49965648 | solution.py:152
  74.2 5.4 copy.62
  84.1 8.0 %reshape.419 = f32[32,128,257]{2,1,0:T(8,128)} reshape(f32[32,32896]{1,0:T(8,128)} %concatenate.36) | data formatting | bytes 8421376 | tf_op jit(solution)/shard_map/while/body/eval_jaxpr/reshape | solution.py:60
  103.7 5.4 copy.62
  113.6 8.0 %reshape.419 = f32[32,128,257]{2,1,0:T(8,128)} reshape(f32[32,32896]{1,0:T(8,128)} %concatenate.36) | data formatting | bytes 8421376 | tf_op jit(solution)/shard_map/while/body/eval_jaxpr/reshape | solution.py:60
  143.2 8.0 %reshape.419 = f32[32,128,257]{2,1,0:T(8,128)} reshape(f32[32,32896]{1,0:T(8,128)} %concatenate.36) | data formatting | bytes 8421376 | tf_op jit(solution)/shard_map/while/body/eval_jaxpr/reshape | solution.py:60
  172.7 8.0 %reshape.419 = f32[32,128,257]{2,1,0:T(8,128)} reshape(f32[32,32896]{1,0:T(8,128)} %concatenate.36) | data formatting | bytes 8421376 | tf_op jit(solution)/shard_map/while/body/eval_jaxpr/reshape | solution.py:60
  202.3 8.0 %reshape.419 = f32[32,128,257]{2,1,0:T(8,128)} reshape(f32[32,32896]{1,0:T(8,128)} %concatenate.36) | data formatting | bytes 8421376 | tf_op jit(solution)/shard_map/while/body/eval_jaxpr/reshape | solution.py:60
  231.8 8.0 %reshape.419 = f32[32,128,257]{2,1,0:T(8,128)} reshape(f32[32,32896]{1,0:T(8,128)} %concatenate.36) | data formatting | bytes 8421376 | tf_op jit(solution)/shard_map/while/body/eval_jaxpr/reshape | solution.py:60
  251.4 5.4 copy.62
  261.4 8.0 %reshape.419 = f32[32,128,257]{2,1,0:T(8,128)} reshape(f32[32,32896]{1,0:T(8,128)} %concatenate.36) | data formatting | bytes 8421376 | tf_op jit(solution)/shard_map/while/body/eval_jaxpr/reshape | solution.py:60
  290.9 8.0 %reshape.419 = f32[32,128,257]{2,1,0:T(8,128)} reshape(f32[32,32896]{1,0:T(8,128)} %concatenate.36) | data formatting | bytes 8421376 | tf_op jit(solution)/shard_map/while/body/eval_jaxpr/reshape | solution.py:60
  320.5 8.0 %reshape.419 = f32[32,128,257]{2,1,0:T(8,128)} reshape(f32[32,32896]{1,0:T(8,128)} %concatenate.36) | data formatting | bytes 8421376 | tf_op jit(solution)/shard_map/while/body/eval_jaxpr/reshape | solution.py:60
  350.0 8.0 %reshape.419 = f32[32,128,257]{2,1,0:T(8,128)} reshape(f32[32,32896]{1,0:T(8,128)} %concatenate.36) | data formatting | bytes 8421376 | tf_op jit(solution)/shard_map/while/body/eval_jaxpr/reshape | solution.py:60
  379.6 8.0 %reshape.419 = f32[32,128,257]{2,1,0:T(8,128)} reshape(f32[32,32896]{1,0:T(8,128)} %concatenate.36) | data formatting | bytes 8421376 | tf_op jit(solution)/shard_map/while/body/eval_jaxpr/reshape | solution.py:60
  409.1 8.0 %reshape.419 = f32[32,128,257]{2,1,0:T(8,128)} reshape(f32[32,32896]{1,0:T(8,128)} %concatenate.36) | data formatting | bytes 8421376 | tf_op jit(solution)/shard_map/while/body/eval_jaxpr/reshape | solution.py:60
  438.6 8.0 %reshape.419 = f32[32,128,257]{2,1,0:T(8,128)} reshape(f32[32,32896]{1,0:T(8,128)} %concatenate.36) | data formatting | bytes 8421376 | tf_op jit(solution)/shard_map/while/body/eval_jaxpr/reshape | solution.py:60
  468.2 8.0 %reshape.419 = f32[32,128,257]{2,1,0:T(8,128)} reshape(f32[32,32896]{1,0:T(8,128)} %concatenate.36) | data formatting | bytes 8421376 | tf_op jit(solution)/shard_map/while/body/eval_jaxpr/reshape | solution.py:60
  497.7 8.0 %reshape.419 = f32[32,128,257]{2,1,0:T(8,128)} reshape(f32[32,32896]{1,0:T(8,128)} %concatenate.36) | data formatting | bytes 8421376 | tf_op jit(solution)/shard_map/while/body/eval_jaxpr/reshape | solution.py:60
  527.3 8.0 %reshape.419 = f32[32,128,257]{2,1,0:T(8,128)} reshape(f32[32,32896]{1,0:T(8,128)} %concatenate.36) | data formatting | bytes 8421376 | tf_op jit(solution)/shard_map/while/body/eval_jaxpr/reshape | solution.py:60
  553.4 8.9 %all-to-all-done.3 = f32[2,128,8]{2,0,1:T(2,128)S(1)} async-done(((f32[2,128,8]{2,0,1:T(2,128)}), f32[2,128,8]{2,0,1:T(2,128)S(1)}, u32[]{:S(2)}, u32[]{:S(2)}) %all-to-all-start.3) | async-done | bytes 8224 | tf_op jit(solution)/shard_map/all_to_all | solution.py:174
  568.8 17.1 %all-to-all-done.2 = f32[2,128,8,128]{3,2,0,1:T(8,128)S(1)} async-done(((f32[2,128,8,128]{3,2,0,1:T(8,128)}), f32[2,128,8,128]{3,2,0,1:T(8,128)S(1)}, u32[]{:S(2)}, u32[]{:S(2)}) %all-to-all-start.2) | async-done | bytes 1048608 | tf_op jit(solution)/shard_map/all_to_all | solution.py:167
  (385 shorter events, 375.5 us)
Async XLA Ops:
  0.6 0.9 copy-start
  1.6 36.2 %copy-start.2 = (f32[256,128]{1,0:T(8,128)S(1)}, f32[256,128]{1,0:T(8,128)}, u32[]{:S(2)}) copy-start(f32[256,128]{1,0:T(8,128)} %param.23) | copy-start | bytes 393220
  4.7 33.7 %copy-start.1 = (f32[128,128]{1,0:T(8,128)S(1)}, f32[128,128]{1,0:T(8,128)}, u32[]{:S(2)}) copy-start(f32[128,128]{1,0:T(8,128)} %param.22) | copy-start | bytes 196612
  39.9 25.7 %copy-start.3 = (f32[4,128]{1,0:T(4,128)S(1)}, f32[4,128]{1,0:T(4,128)}, u32[]{:S(2)}) copy-start(f32[4,128]{1,0:T(4,128)} %param.21) | copy-start | bytes 6148
  39.9 25.7 %copy-start.4 = (s32[512]{0:T(512)S(1)}, s32[512]{0:T(512)}, u32[]{:S(2)}) copy-start(s32[512]{0:T(512)} %param.15) | copy-start | bytes 6148
  39.9 23.5 %all-to-all-start.1 = ((f32[2,128,8,128]{3,2,0,1:T(8,128)}), f32[2,128,8,128]{3,2,0,1:T(8,128)S(1)}, u32[]{:S(2)}, u32[]{:S(2)}) async-start(f32[2,128,8,128]{3,2,0,1:T(8,128)} %pad_maximum_fusion.1), calls=%async_computation.1 | async-start | bytes 2097152 | tf_op jit(solution)/shard_map/all_to_all | solution.py:91
  548.3 14.0 %all-to-all-start.3 = ((f32[2,128,8]{2,0,1:T(2,128)}), f32[2,128,8]{2,0,1:T(2,128)S(1)}, u32[]{:S(2)}, u32[]{:S(2)}) async-start(f32[2,128,8]{2,0,1:T(2,128)} %copy.44), calls=%async_computation.3 | async-start | bytes 262144 | tf_op jit(solution)/shard_map/all_to_all | solution.py:174
  562.3 23.7 %all-to-all-start.2 = ((f32[2,128,8,128]{3,2,0,1:T(8,128)}), f32[2,128,8,128]{3,2,0,1:T(8,128)S(1)}, u32[]{:S(2)}, u32[]{:S(2)}) async-start(f32[2,128,8,128]{3,2,0,1:T(8,128)} %pad_maximum_fusion.2), calls=%async_computation.2 | async-start | bytes 2097152 | tf_op jit(solution)/shard_map/all_to_all | solution.py:167
where the time goes:
time: 593 us; the launch traced here: 588 us
  local copies, waits for them, and re-layouts  316 us (53%)
  other arithmetic  132 us (22%)
  matrix products  59.7 us (10%)
  waiting for transfers between devices  44.9 us (8%)
  blocking collectives  21.6 us (4%)
  starting transfers between devices  12.1 us (2%)
    reshape x16, local copies, waits for them, and re-layouts, diagonal_sums(): skewed = padded.reshape(row_count, tap_count, 2 * tap_count + 1)  128 us
    while x48, local copies, waits for them, and re-layouts  88.2 us
    concatenate x16, local copies, waits for them, and re-layouts, diagonal_sums(): jnp.concatenate([joined, jnp.zeros((row_count, tap_count), jnp.float32)],...  71.9 us
    reduce_sum x16, other arithmetic, diagonal_sums(): column_sums = jnp.sum(skewed, axis=1)  52.8 us
    concatenate x16, other arithmetic, diagonal_sums(): jnp.concatenate([cross_before, cross_now], axis=2)  39.1 us
    all_to_all x1, blocking collectives, body(): lax.all_to_all(requests, ('shot', 'line'), split_axis=1, concat_axis=1, t...  21.6 us
    all_to_all x1, waiting for transfers between devices, body(): lax.all_to_all(values, ('shot', 'line'), split_axis=1, concat_axis=1, til...  18.8 us
    all_to_all x1, waiting for transfers between devices, body(): lax.all_to_all(send_grad.reshape(2, device_count, slot_cap, tap_count), (...  17.1 us
  transfers between devices with their start and end apart: 3, of which 3 were waited for; matrix products, arithmetic and copies ran while one was open for 1% of the time, Pallas kernels for 0%

commit v1 on v0

v1 whole, which is shorter than its diff:
```python
import jax
import jax.numpy as jnp
import numpy as np
import ml_dtypes
from jax import lax
from jax.experimental import pallas as pl
from jax.experimental.pallas import tpu as pltpu
from jax.sharding import PartitionSpec as P

AXES = ("shot", "line")
DEVS = 128
ROWS = 512
NS = 2048
TAPS = 128
CAP = 8
PAIR = 2 * CAP
SLOTS = DEVS * PAIR
RCV = 128
CMP = 256
SRC = 4
WIN = 256
BLOCKS = NS // TAPS
ROWBLK = 128
step_size = 0.5
f32, bf16, i32 = jnp.float32, jnp.bfloat16, jnp.int32
NT = (((1,), (1,)), ((), ()))
MIB = 1024 * 1024


def split_pair(matrix):
    high = matrix.astype(ml_dtypes.bfloat16)
    low = (matrix - high.astype(np.float64)).astype(ml_dtypes.bfloat16)
    return high, low


def make_tables():
    angle = 2.0 * np.pi * (np.arange(TAPS) + 0.5) / WIN
    place = np.arange(WIN)
    phase = place[:, None] * angle[None, :]
    forward = np.concatenate([np.cos(phase), -np.sin(phase)], axis=1)
    inverse = forward.T / TAPS
    lag_phase = np.arange(TAPS)[:, None] * angle[None, :]
    even = 2.0 * np.cos(lag_phase)
    even[0] = 1.0
    f_high, f_low = split_pair(forward)
    d_pair = np.concatenate(split_pair(forward[:TAPS]), axis=0)
    e_pair = np.concatenate(split_pair(forward[TAPS:]), axis=0)
    i_pair = np.concatenate(split_pair(inverse[:, :TAPS]), axis=1)
    c_pair = np.concatenate(split_pair(even), axis=1)
    tail = split_pair(inverse[:, TAPS:] @ forward[TAPS:])[0]
    f_pair = np.concatenate([f_high, f_low], axis=0)
    return dict(f=f_pair, d=d_pair, e=e_pair, i=i_pair, c=c_pair, tail=tail)


def two(values):
    high = values.astype(bf16)
    low = (values - high.astype(f32)).astype(bf16)
    return high, low


def mm(a, b):
    return jnp.dot(a, b, preferred_element_type=f32)


def iota(shape, dim):
    return lax.broadcasted_iota(i32, shape, dim)


def as_bf16(mask):
    return mask.astype(f32).astype(bf16)


def fine_mm(values, pair):
    width = pair.shape[1] // 2
    high, low = two(values)
    both = mm(high, pair)
    return both[:, :width] + (both[:, width:] + mm(low, pair[:, :width]))


def plan_kernel(count_ref, rterm_ref, cterm_ref, rhome_ref, chome_ref, traces_hbm,
                pay_ref, slot_ref, tbuf, sems):
    copies = []
    for j in range(4):
        part = pl.ds(j * 128, 128)
        copies.append(pltpu.make_async_copy(traces_hbm.at[part], tbuf.at[part], sems.at[j]))
        copies[-1].start()
    before_mask = as_bf16(iota((ROWS, ROWS), 0) < iota((ROWS, ROWS), 1))

    def look_up(term, home, bits):
        high, low = term >> 7, term & 127
        owner_t = jnp.transpose((home >> bits).astype(f32)).astype(bf16)
        place_t = jnp.transpose((home & (2 ** bits - 1)).astype(f32)).astype(bf16)
        pick_high = as_bf16(iota((home.shape[0], ROWS), 0) == high)
        pick_low = iota((128, ROWS), 0) == low
        owner = jnp.sum(jnp.where(pick_low, mm(owner_t, pick_high), 0.0), axis=0, keepdims=True)
        place = jnp.sum(jnp.where(pick_low, mm(place_t, pick_high), 0.0), axis=0, keepdims=True)
        mine = iota((DEVS, ROWS), 0) == owner.astype(i32)
        mine16 = as_bf16(mine)
        before = mm(mine16, before_mask)
        rank = jnp.sum(jnp.where(mine, before, 0.0), axis=0, keepdims=True)
        return owner, place, rank, mine16

    r_owner, r_place, r_rank, r_mine = look_up(rterm_ref[...], rhome_ref[...], 7)
    c_owner, c_place, c_rank, c_mine = look_up(cterm_ref[...], chome_ref[...], 8)
    live = (iota((1, ROWS), 1) < count_ref[0]).astype(f32)
    r_slot = r_owner * PAIR + r_rank
    c_slot = c_owner * PAIR + (c_rank + CAP)
    powers = []
    for j in range(4):
        copies[j].wait()
        total = jnp.zeros((128, 128), f32)
        for b in range(BLOCKS):
            x = tbuf[j * 128:(j + 1) * 128, b * 128:(b + 1) * 128].astype(f32)
            total = total + x * x
        powers.append(jnp.sum(jnp.transpose(total), axis=0, keepdims=True))
    power = jnp.concatenate(powers, axis=1) * live
    p_high, p_low = two(power)
    p_high, p_low = p_high.astype(f32), p_low.astype(f32)
    line = iota((2 * PAIR, ROWS), 0).astype(f32)

    def weights(rank, place):
        at_place = jnp.where(line == rank, place, 0.0)
        here = line == rank + PAIR
        return ((at_place + jnp.where(here, p_high, 0.0)).astype(bf16),
                jnp.where(here, p_low, 0.0).astype(bf16))

    pay = jnp.zeros((DEVS, 2 * PAIR), f32)
    for mine, rank, place in ((r_mine, r_rank, r_place), (c_mine, c_rank + CAP, c_place)):
        for weight in weights(rank, place):
            pay = pay + lax.dot_general(mine, weight, NT, preferred_element_type=f32)
    pay_ref[...] = pay
    slot_ref[...] = jnp.concatenate(
        [r_slot, c_slot, live, power, jnp.zeros((4, ROWS), f32)], axis=0)


def pick_kernel(got_ref, rcv_ref, cmp_ref, out_ref):
    got = got_ref[...].astype(bf16)
    table = jnp.concatenate([rcv_ref[...], cmp_ref[...]], axis=0)
    pair = jnp.concatenate(two(table), axis=1)
    chunk = 512
    ones = jnp.ones((2 * PAIR, 128), bf16)
    for c in range(SLOTS // chunk):
        spread = as_bf16((iota((chunk, DEVS), 0) + c * chunk) >> 4 == iota((chunk, DEVS), 1))
        line = mm(spread, got)
        keep = iota((chunk, 2 * PAIR), 1) == (iota((chunk, 2 * PAIR), 0) & (PAIR - 1))
        place = mm(jnp.where(keep, line, 0.0).astype(bf16), ones).astype(i32)
        place = place + ((iota((chunk, 128), 0) & CAP) << 4)
        lane = iota((chunk, 128), 1)
        pick = jnp.concatenate([as_bf16(place == lane + k * 128) for k in range(3)], axis=1)
        both = mm(pick, pair)
        out_ref[c * chunk:(c + 1) * chunk, :] = both[:, :TAPS] + both[:, TAPS:]


def lags_kernel(after_ref, traces_ref, targets_ref, f_ref, e_ref, i_ref, c_ref, d_ref,
                even_ref, base_ref, last_ref):
    f_high, f_low = f_ref[:WIN, :], f_ref[WIN:, :]
    e_pair = e_ref[...]
    own = jnp.zeros((ROWBLK, WIN), f32)
    cross = jnp.zeros((ROWBLK, WIN), f32)
    for b in range(BLOCKS):
        now = traces_ref[:, b * 128:(b + 1) * 128]
        goal = targets_ref[:, b * 128:(b + 1) * 128]
        u = mm(jnp.concatenate([now, now], axis=1), e_pair)
        v = mm(jnp.concatenate([goal, goal], axis=1), e_pair)
        if b == 0:
            x = u
        else:
            window = traces_ref[:, (b - 1) * 128:(b + 1) * 128]
            x = mm(window, f_high) + mm(window, f_low)
        xr, xi = x[:, :TAPS], x[:, TAPS:]
        flip = jnp.concatenate([xi, -xr], axis=1)
        for_re = jnp.concatenate([xr, xr], axis=1)
        ur, ui = u[:, :TAPS], u[:, TAPS:]
        vr, vi = v[:, :TAPS], v[:, TAPS:]
        own = own + jnp.concatenate([xr * ur + xi * ui, xr * ui - xi * ur], axis=1)
        cross = cross + jnp.concatenate([xr * vr + xi * vi, xr * vi - xi * vr], axis=1)
    i_pair = i_ref[...]
    even_ref[...] = fine_mm(fine_mm(own, i_pair), c_ref[...])
    base_ref[...] = fine_mm(cross, i_pair)
    final = traces_ref[:, (BLOCKS - 1) * 128:]
    last_ref[...] = mm(jnp.concatenate([final, final], axis=1), d_ref[...])


def books_kernel(got_ref, slot_ref, srcloc_ref, place_ref, energy_ref, col_ref):
    got = jnp.concatenate([got_ref[...], jnp.zeros((DEVS, 128 - 2 * PAIR), f32)], axis=1)
    turned = jnp.transpose(got)[:2 * PAIR]
    first = turned.astype(bf16)
    rest = turned - first.astype(f32)
    second = rest.astype(bf16)
    third = (rest - second.astype(f32)).astype(bf16)
    q = iota((DEVS, SLOTS), 1)
    spread = as_bf16((q >> 4) == iota((DEVS, SLOTS), 0))
    wide = mm(first, spread) + (mm(second, spread) + mm(third, spread))
    line = iota((PAIR, SLOTS), 0)
    slot = iota((PAIR, SLOTS), 1) & (PAIR - 1)
    place = jnp.sum(jnp.where(line == slot, wide[:PAIR], 0.0), axis=0, keepdims=True)
    power = jnp.sum(jnp.where(line == slot, wide[PAIR:], 0.0), axis=0, keepdims=True)
    place = place.astype(i32) + ((iota((1, SLOTS), 1) & CAP) << 4)
    place_ref[...] = jnp.broadcast_to(place, (8, SLOTS))
    for c in range(3):
        rows = iota((128, SLOTS), 0) + c * 128
        energy = jnp.sum(jnp.where(rows == place, power, 0.0), axis=1, keepdims=True)
        energy_ref[c * 128:(c + 1) * 128, :] = jnp.broadcast_to(
            step_size / jnp.maximum(energy, 1.0), (128, 128))
    lines = jnp.concatenate(
        [slot_ref[...], srcloc_ref[...].astype(f32), jnp.zeros((128 - 9, ROWS), f32)], axis=0)
    for j in range(4):
        col_ref[j * 128:(j + 1) * 128, :] = jnp.transpose(lines[:, j * 128:(j + 1) * 128])


def grad_kernel(fetched_ref, col_ref, slot_ref, srcloc_ref, src_ref, even_ref, base_ref,
                last_ref, d_ref, tail_ref, i_ref, out_ref, src_out_ref):
    col = col_ref[...]
    r_slot = col[:, 0:1].astype(i32)
    c_slot = col[:, 1:2].astype(i32)
    live = col[:, 2:3]
    src_local = col[:, 8:9]
    src = src_ref[...]
    mixed = jnp.zeros((ROWS, TAPS), f32)
    for s in range(SRC):
        mixed = jnp.where(src_local == float(s), src[s:s + 1, :], mixed)
    width = 256
    lane = iota((ROWS, width), 1)
    both = jnp.zeros((ROWS, 2 * TAPS), f32)
    for k in range(SLOTS // width):
        at = lane + k * width
        pick = as_bf16((at == r_slot) | (at == c_slot))
        rows = jnp.concatenate(two(fetched_ref[k * width:(k + 1) * width, :]), axis=1)
        both = both + mm(pick, rows)
    mixed = (mixed + (both[:, :TAPS] + both[:, TAPS:])).astype(bf16)
    h = mm(jnp.concatenate([mixed, mixed], axis=1), d_ref[...])
    hr, hi = h[:, :TAPS], h[:, TAPS:]
    xr, xi = last_ref[:, :TAPS], last_ref[:, TAPS:]
    past = jnp.concatenate([xr * hr - xi * hi, xr * hi + xi * hr], axis=1)
    m = mm(past.astype(bf16), tail_ref[...])
    mr, mi = m[:, :TAPS], m[:, TAPS:]
    even = even_ref[...]
    spectrum = jnp.concatenate(
        [even * hr - (xr * mr + xi * mi), even * hi - (xr * mi - xi * mr)], axis=1)
    grad = (fine_mm(spectrum, i_ref[...]) - base_ref[...]) * live
    rows = jnp.concatenate(two(grad), axis=1)
    lines = slot_ref[...]
    r_line, c_line, power = lines[0:1].astype(i32), lines[1:2].astype(i32), lines[3:4]
    chunk = 512
    for k in range(SLOTS // chunk):
        at = iota((chunk, ROWS), 0) + k * chunk
        place = as_bf16((at == r_line) | (at == c_line))
        both = mm(place, rows)
        out_ref[k * chunk:(k + 1) * chunk, :] = both[:, :TAPS] + both[:, TAPS:]
    mine = iota((8, ROWS), 0) == srcloc_ref[...]
    both = mm(as_bf16(mine), rows)
    energy = jnp.sum(jnp.where(mine, power, 0.0), axis=1, keepdims=True)
    change = step_size * (both[:, :TAPS] + both[:, TAPS:]) / jnp.maximum(energy, 1.0)
    src_out_ref[...] = src - change[:SRC]


def settle_kernel(grads_ref, place_ref, energy_ref, rcv_ref, cmp_ref, rcv_out_ref, cmp_out_ref):
    place = place_ref[0:1, :]
    total = jnp.zeros((RCV + CMP, 2 * TAPS), f32)
    width = 256
    for k in range(SLOTS // width):
        rows = jnp.concatenate(two(grads_ref[k * width:(k + 1) * width, :]), axis=1)
        pick = as_bf16(iota((RCV + CMP, width), 0) == place[:, k * width:(k + 1) * width])
        total = total + mm(pick, rows)
    change = (total[:, :TAPS] + total[:, TAPS:]) * energy_ref[...]
    rcv_out_ref[...] = rcv_ref[...] - change[:RCV]
    cmp_out_ref[...] = cmp_ref[...] - change[RCV:]


def shape(*dims, dtype=f32):
    return jax.ShapeDtypeStruct(dims, dtype)


VM = pl.BlockSpec(memory_space=pltpu.VMEM)
SM = pl.BlockSpec(memory_space=pltpu.SMEM)
params = pltpu.CompilerParams(vmem_limit_bytes=40 * MIB)


def body(traces, targets, src_local, rcv_term, cmp_term, rcv_home, cmp_home, counts,
         src_filters, rcv_filters, cmp_filters):
    tables = {name: jnp.asarray(value) for name, value in make_tables().items()}
    src_line = src_local.reshape(1, ROWS)
    pay, slot_lines = pl.pallas_call(
        plan_kernel,
        out_shape=(shape(DEVS, 2 * PAIR), shape(8, ROWS)),
        in_specs=[SM, VM, VM, VM, VM, pl.BlockSpec(memory_space=pl.ANY)],
        out_specs=(VM, VM),
        scratch_shapes=[pltpu.VMEM((ROWS, NS), bf16), pltpu.SemaphoreType.DMA((4,))],
        compiler_params=params,
        name="plan",
    )(counts, rcv_term.reshape(1, ROWS), cmp_term.reshape(1, ROWS),
      rcv_home.reshape(-1, 128), cmp_home.reshape(-1, 128), traces)
    got = lax.all_to_all(pay, AXES, split_axis=0, concat_axis=0, tiled=True)
    values = pl.pallas_call(
        pick_kernel,
        out_shape=shape(SLOTS, TAPS),
        in_specs=[VM] * 3, out_specs=VM,
        compiler_params=params,
        name="pick",
    )(got, rcv_filters, cmp_filters)
    fetched = lax.all_to_all(values.reshape(DEVS, PAIR, TAPS), AXES, split_axis=0, concat_axis=0,
                             tiled=True).reshape(SLOTS, TAPS)

    def whole(array):
        return pl.BlockSpec(array.shape, lambda i: (0, 0))

    def blk(width):
        return pl.BlockSpec((ROWBLK, width), lambda i: (i, 0))

    even, base, last = pl.pallas_call(
        lags_kernel,
        grid=(ROWS // ROWBLK,),
        out_shape=(shape(ROWS, TAPS), shape(ROWS, TAPS), shape(ROWS, WIN)),
        in_specs=[pl.BlockSpec((8, 2 * PAIR), lambda i: (0, 0)), blk(NS), blk(NS)]
        + [whole(tables[n]) for n in "feicd"],
        out_specs=(blk(TAPS), blk(TAPS), blk(WIN)),
        compiler_params=params,
        cost_estimate=pl.CostEstimate(flops=5 * 10 ** 9, bytes_accessed=5 * 10 ** 6,
                                      transcendentals=0),
        name="lags",
    )(got, traces, targets, *[tables[n] for n in "feicd"])
    place, energy, cols = pl.pallas_call(
        books_kernel,
        out_shape=(shape(8, SLOTS, dtype=i32), shape(RCV + CMP, 128), shape(ROWS, 128)),
        in_specs=[VM] * 3, out_specs=(VM,) * 3,
        compiler_params=params,
        name="books",
    )(got, slot_lines, src_line)
    send, src_out = pl.pallas_call(
        grad_kernel,
        out_shape=(shape(SLOTS, TAPS), shape(SRC, TAPS)),
        in_specs=[VM] * 11, out_specs=(VM, VM),
        compiler_params=params,
        name="grad",
    )(fetched, cols, slot_lines, src_line, src_filters, even, base, last,
      tables["d"], tables["tail"], tables["i"])
    back = lax.all_to_all(send.reshape(DEVS, PAIR, TAPS), AXES, split_axis=0, concat_axis=0,
                          tiled=True).reshape(SLOTS, TAPS)
    rcv_out, cmp_out = pl.pallas_call(
        settle_kernel,
        out_shape=(shape(RCV, TAPS), shape(CMP, TAPS)),
        in_specs=[VM] * 5, out_specs=(VM, VM),
        compiler_params=params,
        name="settle",
    )(back, place, energy, rcv_filters, cmp_filters)
    return src_out, rcv_out, cmp_out


def solution(mesh):
    rows = P(AXES, None)
    flat = P(AXES)
    return jax.shard_map(
        body,
        mesh=mesh,
        in_specs=(rows, rows, flat, flat, flat, P(), P(), flat, rows, rows, rows),
        out_specs=(rows, rows, rows),
        check_vma=False,
    )
```

time: 593 us -> 95.3 us (0.16)
  local copies, waits for them, and re-layouts: 316 us -> 21.8 us
  other arithmetic: 132 us -> 0 us
  matrix products: 59.7 us -> 0 us
  waiting for transfers between devices: 44.9 us -> 1.47 us
  blocking collectives: 21.6 us -> 48.5 us
  Pallas kernels: 0 us -> 17.1 us
  starting transfers between devices: 12.1 us -> 4.21 us
    reshape x16 -> x0, local copies, waits for them, and re-layouts: 128 us -> none  [diagonal_sums(): skewed = padded.reshape(row_count, tap_count, 2 * tap_count + 1)]
    while x48 -> x0, local copies, waits for them, and re-layouts: 88.2 us -> none
    concatenate x16 -> x0, local copies, waits for them, and re-layouts: 71.9 us -> none  [diagonal_sums(): jnp.concatenate([joined, jnp.zeros((row_count, tap_count), jnp.float32)],...]
    reduce_sum x34 -> x0, other arithmetic: 69.9 us -> none  [the longest x16 52.8 us: diagonal_sums(): column_sums = jnp.sum(skewed, axis=1)]
    dot_general x105 -> x0, matrix products: 59.7 us -> none  [the longest x16 11.2 us: one_block(): jnp.einsum('rk,kji->rji', filter_block, shift_upper, preferred_element_ty...]
    all_to_all x3 -> x1, waiting for transfers between devices: 44.9 us -> 1.47 us  [body(): lax.all_to_all(values.reshape(DEVS, PAIR, TAPS), AXES, split_axis=0, conc...]
    concatenate x16 -> x0, other arithmetic: 39.1 us -> none  [diagonal_sums(): jnp.concatenate([cross_before, cross_now], axis=2)]
    all_to_all x1 -> x2, blocking collectives: 21.6 us -> 48.5 us  [the longest x1 27.6 us: body(): lax.all_to_all(send.reshape(DEVS, PAIR, TAPS), AXES, split_axis=0, concat...]
  transfers between devices with their start and end apart: 3 -> 1, of which waited for: 3 -> 1; matrix products, arithmetic and copies ran while one was open for 1% -> 0% of each run, Pallas kernels for 0% -> 8%
where the time goes in v1:
time: 95.3 us; the launch traced here: 94.6 us
  blocking collectives  48.5 us (51%)
  local copies, waits for them, and re-layouts  21.8 us (23%)
  Pallas kernels  17.1 us (18%)
  starting transfers between devices  4.21 us (4%)
  waiting for transfers between devices  1.47 us (2%)
  between operations  1.39 us (1%)
    all_to_all x1, blocking collectives, body(): lax.all_to_all(send.reshape(DEVS, PAIR, TAPS), AXES, split_axis=0, concat...  27.6 us
    unnamed x62, local copies, waits for them, and re-layouts  21.8 us
    all_to_all x1, blocking collectives, body(): got = lax.all_to_all(pay, AXES, split_axis=0, concat_axis=0, tiled=True)  20.9 us
    pallas_call x1, Pallas kernels, body(): pl.pallas_call(lags_kernel, grid=(ROWS // ROWBLK,), out_shape=(shape(ROWS...  6.99 us
    all_to_all x1, starting transfers between devices, body(): lax.all_to_all(values.reshape(DEVS, PAIR, TAPS), AXES, split_axis=0, conc...  4.21 us
    pallas_call x1, Pallas kernels, body(): pl.pallas_call(grad_kernel, out_shape=(shape(SLOTS, TAPS), shape(SRC, TAP...  3.52 us
    pallas_call x1, Pallas kernels, body(): pl.pallas_call(pick_kernel, out_shape=shape(SLOTS, TAPS), in_specs=[VM] *...  2.36 us
    pallas_call x1, Pallas kernels, body(): pl.pallas_call(plan_kernel, out_shape=(shape(DEVS, 2 * PAIR), shape(8, RO...  2.07 us
  transfers between devices with their start and end apart: 1, of which 1 were waited for; matrix products, arithmetic and copies ran while one was open for 0% of the time, Pallas kernels for 8%

profile of v1, /device:TPU:1, one launch (start us, length us, event | category | flops | bytes accessed | tf_op | source)
XLA Modules:
  0.0 94.6 jit_solution(6528869744820456727)
XLA Ops:
  1.3 1.6 %copy-done = bf16[512,2048]{1,0:T(8,128)(2,1)S(1)} copy-done((bf16[512,2048]{1,0:T(8,128)(2,1)S(1)}, bf16[512,2048]{1,0:T(8,128)(2,1)}, u32[]{:S(2)}) %copy-start) | copy-done | bytes 2097176
  2.9 0.9 copy-done.14
  3.8 0.8 copy-done.19
  6.0 2.1 %plan.1 = (f32[128,32]{1,0:T(8,128)S(1)}, f32[8,512]{1,0:T(8,128)S(1)}) custom-call(s32[1]{0:T(128)S(6)} %copy.21.count_ref, s32[1,512]{1,0:T(1,128)S(1)} %bitcast.24, s32[1,512]{1,0:T(1,128)S(1)} %bitcast.25, s32[128,128]{1,0:T(8,128)S(1)} %bitcast.20, s32[256,128]{1,0:T(8,128)S(1)} %bitcast.19, bf16[512,2048]{1,0:T(8,128)(2,1)S(1)} %copy-done), custom_call_target="tpu_custom_call" | custom-call | tf_op jit(solution)/shard_map/plan/pallas_call | solution.py:283
  8.1 20.9 %all_to_all.21 = f32[128,1,32]{2,1,0:T(1,128)S(1)} all-to-all(f32[128,1,32]{2,1,0:T(1,128)S(1)} %bitcast.21), channel_id=1, replica_groups=mesh['shot'=32,'line'=4] {'shot','line'}, dimensions={0} | all-to-all | bytes 32768 | tf_op jit(solution)/shard_map/all_to_all | solution.py:293
  29.0 2.4 %pick.1 = f32[2048,128]{1,0:T(8,128)} custom-call(f32[128,32]{1,0:T(8,128)S(1)} %bitcast.16, f32[128,128]{1,0:T(8,128)S(1)} %copy-done.5, f32[256,128]{1,0:T(8,128)S(1)} %copy-done.2), custom_call_target="tpu_custom_call" | custom-call | tf_op jit(solution)/shard_map/pick/pallas_call | solution.py:294
  31.4 4.2 %all-to-all-start.1 = ((f32[128,16,128]{2,1,0:T(8,128)}), f32[128,16,128]{2,1,0:T(8,128)S(1)}, u32[]{:S(2)}, u32[]{:S(2)}) async-start(f32[128,16,128]{2,1,0:T(8,128)} %bitcast.7), calls=%async_computation.1 | async-start | bytes 2097152 | tf_op jit(solution)/shard_map/all_to_all | solution.py:301
  36.3 0.9 books.1
  39.3 0.9 copy-done.16
  40.2 1.6 %copy-done.27 = bf16[512,2048]{1,0:T(8,128)(2,1)S(1)} copy-done((bf16[512,2048]{1,0:T(8,128)(2,1)S(1)}, bf16[512,2048]{1,0:T(8,128)(2,1)}, u32[]{:S(2)}) %copy-start.27) | copy-done | bytes 2097176
  41.8 0.9 %copy-done.28 = bf16[512,256]{1,0:T(8,128)(2,1)S(1)} copy-done((bf16[512,256]{1,0:T(8,128)(2,1)S(1)}, bf16[512,256]{1,0:T(8,128)(2,1)}, u32[]{:S(2)}) %copy-start.28) | copy-done | bytes 262168
  42.7 0.9 copy-done.29
  43.6 0.8 copy-done.30
  44.5 7.0 %lags.1 = (f32[512,128]{1,0:T(8,128)S(1)}, f32[512,128]{1,0:T(8,128)S(1)}, f32[512,256]{1,0:T(8,128)S(1)}) custom-call(f32[128,32]{1,0:T(8,128)S(1)} %bitcast.18, bf16[512,2048]{1,0:T(8,128)(2,1)S(1)} %copy-done.1, bf16[512,2048]{1,0:T(8,128)(2,1)S(1)} %copy-done.27, bf16[512,256]{1,0:T(8,128)(2,1)S(1)} %copy-done.28, bf16[256,256]{1,0:T(8,128)(2,1)S(1)} %copy-done.29, ...), custom_call_target="tpu_custom_call" | custom-call | flops 5000000000 | bytes 5000000 | tf_op jit(solution)/shard_map/lags/pallas_call | solution.py:310
  53.7 1.5 %all-to-all-done.1 = f32[128,16,128]{2,1,0:T(8,128)S(1)} async-done(((f32[128,16,128]{2,1,0:T(8,128)}), f32[128,16,128]{2,1,0:T(8,128)S(1)}, u32[]{:S(2)}, u32[]{:S(2)}) %all-to-all-start.1) | async-done | bytes 1048608 | tf_op jit(solution)/shard_map/all_to_all | solution.py:301
  55.1 1.0 %copy-done.4 = f32[512,256]{1,0:T(8,128)S(1)} copy-done((f32[512,256]{1,0:T(8,128)S(1)}, f32[512,256]{1,0:T(8,128)}, u32[]{:S(2)}) %copy-start.4) | copy-done | bytes 524312
  56.2 0.9 %copy-done.7 = f32[512,128]{1,0:T(8,128)S(1)} copy-done((f32[512,128]{1,0:T(8,128)S(1)}, f32[512,128]{1,0:T(8,128)}, u32[]{:S(2)}) %copy-start.7) | copy-done | bytes 262168
  57.1 0.9 %copy-done.9 = f32[512,128]{1,0:T(8,128)S(1)} copy-done((f32[512,128]{1,0:T(8,128)S(1)}, f32[512,128]{1,0:T(8,128)}, u32[]{:S(2)}) %copy-start.9) | copy-done | bytes 262168
  58.1 0.9 %copy-done.11 = f32[512,128]{1,0:T(8,128)S(1)} copy-done((f32[512,128]{1,0:T(8,128)S(1)}, f32[512,128]{1,0:T(8,128)}, u32[]{:S(2)}) %copy-start.11) | copy-done | bytes 262168
  59.0 0.9 copy-done.17
  59.9 0.9 copy-done.18
  62.2 3.5 %grad.1 = (f32[2048,128]{1,0:T(8,128)S(1)}, f32[4,128]{1,0:T(4,128)}) custom-call(f32[2048,128]{1,0:T(8,128)S(1)} %bitcast.13, f32[512,128]{1,0:T(8,128)S(1)} %copy-done.7, f32[8,512]{1,0:T(8,128)S(1)} %get-tuple-element.16.slot_ref, s32[1,512]{1,0:T(1,128)S(1)} %bitcast.23, f32[4,128]{1,0:T(4,128)S(1)} %copy-done.26, f32[512,128]{1,0:T(8,128)S(1)} %copy-done.9, ...), custom_call_target="tpu_custom_call" | custom-call | tf_op jit(solution)/shard_map/grad/pallas_call | solution.py:329
  65.7 27.6 %all_to_all.22 = f32[128,16,128]{2,1,0:T(8,128)S(1)} all-to-all(f32[128,16,128]{2,1,0:T(8,128)S(1)} %bitcast.15), channel_id=1, replica_groups=mesh['shot'=32,'line'=4] {'shot','line'}, dimensions={0} | all-to-all | bytes 2097152 | tf_op jit(solution)/shard_map/all_to_all | solution.py:337
  93.3 1.2 %settle.1 = (f32[128,128]{1,0:T(8,128)}, f32[256,128]{1,0:T(8,128)}) custom-call(f32[2048,128]{1,0:T(8,128)S(1)} %bitcast.14, s32[8,2048]{1,0:T(8,128)S(1)} %copy-done.21, f32[384,128]{1,0:T(8,128)S(1)} %copy-done.13, f32[128,128]{1,0:T(8,128)S(1)} %copy-done.5, f32[256,128]{1,0:T(8,128)S(1)} %copy-done.2), custom_call_target="tpu_custom_call" | custom-call | tf_op jit(solution)/shard_map/settle/pallas_call | solution.py:339
  (48 shorter events, 7.7 us)
Async XLA Ops:
  1.3 1.6 %copy-start = (bf16[512,2048]{1,0:T(8,128)(2,1)S(1)}, bf16[512,2048]{1,0:T(8,128)(2,1)}, u32[]{:S(2)}) copy-start(bf16[512,2048]{1,0:T(8,128)(2,1)} %traces_ref.1) | copy-start | bytes 6291460
  2.9 0.9 copy-start.14
  3.8 0.8 copy-start.19
  6.0 23.1 %copy-start.2 = (f32[256,128]{1,0:T(8,128)S(1)}, f32[256,128]{1,0:T(8,128)}, u32[]{:S(2)}) copy-start(f32[256,128]{1,0:T(8,128)} %cmp_ref.3) | copy-start | bytes 393220
  6.0 23.1 %copy-start.5 = (f32[128,128]{1,0:T(8,128)S(1)}, f32[128,128]{1,0:T(8,128)}, u32[]{:S(2)}) copy-start(f32[128,128]{1,0:T(8,128)} %rcv_ref.3) | copy-start | bytes 196612
  8.1 31.2 %copy-start.1 = (bf16[512,2048]{1,0:T(8,128)(2,1)S(1)}, bf16[512,2048]{1,0:T(8,128)(2,1)}, u32[]{:S(2)}) copy-start(bf16[512,2048]{1,0:T(8,128)(2,1)} %traces_ref.1) | copy-start | bytes 6291460
  8.1 31.2 %copy-start.15 = (bf16[256,256]{1,0:T(8,128)(2,1)S(1)}, bf16[256,256]{1,0:T(8,128)(2,1)}, u32[]{:S(2)}) copy-start(bf16[256,256]{1,0:T(8,128)(2,1)} %constant.15.clone.i_ref) | copy-start | bytes 393220
  31.4 23.7 %all-to-all-start.1 = ((f32[128,16,128]{2,1,0:T(8,128)}), f32[128,16,128]{2,1,0:T(8,128)S(1)}, u32[]{:S(2)}, u32[]{:S(2)}) async-start(f32[128,16,128]{2,1,0:T(8,128)} %bitcast.7), calls=%async_computation.1 | async-start | bytes 2097152 | tf_op jit(solution)/shard_map/all_to_all | solution.py:301
  37.2 0.7 copy-start.6
  39.3 0.9 copy-start.16
  40.2 1.6 %copy-start.27 = (bf16[512,2048]{1,0:T(8,128)(2,1)S(1)}, bf16[512,2048]{1,0:T(8,128)(2,1)}, u32[]{:S(2)}) copy-start(bf16[512,2048]{1,0:T(8,128)(2,1)} %targets_ref.1) | copy-start | bytes 6291460
  41.8 0.9 %copy-start.28 = (bf16[512,256]{1,0:T(8,128)(2,1)S(1)}, bf16[512,256]{1,0:T(8,128)(2,1)}, u32[]{:S(2)}) copy-start(bf16[512,256]{1,0:T(8,128)(2,1)} %constant.12.clone.f_ref) | copy-start | bytes 786436
  42.7 0.9 copy-start.29
  43.6 0.8 copy-start.30
  51.5 0.8 copy-start.3
  52.9 0.7 copy-start.10
  55.1 1.0 %copy-start.4 = (f32[512,256]{1,0:T(8,128)S(1)}, f32[512,256]{1,0:T(8,128)}, u32[]{:S(2)}) copy-start(f32[512,256]{1,0:T(8,128)} %copy-done.3) | copy-start | bytes 1572868
  56.2 0.9 %copy-start.7 = (f32[512,128]{1,0:T(8,128)S(1)}, f32[512,128]{1,0:T(8,128)}, u32[]{:S(2)}) copy-start(f32[512,128]{1,0:T(8,128)} %copy-done.6) | copy-start | bytes 786436
  57.1 0.9 %copy-start.9 = (f32[512,128]{1,0:T(8,128)S(1)}, f32[512,128]{1,0:T(8,128)}, u32[]{:S(2)}) copy-start(f32[512,128]{1,0:T(8,128)} %copy-done.8) | copy-start | bytes 786436
  58.1 0.9 %copy-start.11 = (f32[512,128]{1,0:T(8,128)S(1)}, f32[512,128]{1,0:T(8,128)}, u32[]{:S(2)}) copy-start(f32[512,128]{1,0:T(8,128)} %copy-done.10) | copy-start | bytes 786436
  59.0 0.9 copy-start.17
  59.9 0.9 copy-start.18
  62.2 31.1 %copy-start.13 = (f32[384,128]{1,0:T(8,128)S(1)}, f32[384,128]{1,0:T(8,128)}, u32[]{:S(2)}) copy-start(f32[384,128]{1,0:T(8,128)} %copy-done.12) | copy-start | bytes 589828
  62.2 31.1 %copy-start.21 = (s32[8,2048]{1,0:T(8,128)S(1)}, s32[8,2048]{1,0:T(8,128)}, u32[]{:S(2)}) copy-start(s32[8,2048]{1,0:T(8,128)} %copy-done.20) | copy-start | bytes 196612
  (8 other events, 5.4 us)

commit v2 on v1

v2 whole, which is shorter than its diff:
```python
import jax
import jax.numpy as jnp
import numpy as np
import ml_dtypes
from jax import lax
from jax.experimental import pallas as pl
from jax.experimental.pallas import tpu as pltpu
from jax.sharding import PartitionSpec as P

AXES = ("shot", "line")
DEVS = 128
ROWS = 512
NS = 2048
TAPS = 128
CAP = 8
PAIR = 2 * CAP
SLOTS = DEVS * PAIR
RCV = 128
CMP = 256
SRC = 4
WIN = 256
BLOCKS = NS // TAPS
ROWBLK = 128
step_size = 0.5
f32, bf16, i32 = jnp.float32, jnp.bfloat16, jnp.int32
NT = (((1,), (1,)), ((), ()))
MIB = 1024 * 1024


def split_pair(matrix):
    high = matrix.astype(ml_dtypes.bfloat16)
    low = (matrix - high.astype(np.float64)).astype(ml_dtypes.bfloat16)
    return high, low


def make_tables():
    angle = 2.0 * np.pi * (np.arange(TAPS) + 0.5) / WIN
    place = np.arange(WIN)
    phase = place[:, None] * angle[None, :]
    forward = np.concatenate([np.cos(phase), -np.sin(phase)], axis=1)
    inverse = forward.T / TAPS
    lag_phase = np.arange(TAPS)[:, None] * angle[None, :]
    even = 2.0 * np.cos(lag_phase)
    even[0] = 1.0
    f_high, f_low = split_pair(forward)
    d_pair = np.concatenate(split_pair(forward[:TAPS]), axis=0)
    e_pair = np.concatenate(split_pair(forward[TAPS:]), axis=0)
    i_pair = np.concatenate(split_pair(inverse[:, :TAPS]), axis=1)
    c_pair = np.concatenate(split_pair(even), axis=1)
    tail = split_pair(inverse[:, TAPS:] @ forward[TAPS:])[0]
    f_pair = np.concatenate([f_high, f_low], axis=0)
    return dict(f=f_pair, d=d_pair, e=e_pair, i=i_pair, c=c_pair, tail=tail)


def two(values):
    high = values.astype(bf16)
    low = (values - high.astype(f32)).astype(bf16)
    return high, low


def mm(a, b):
    return jnp.dot(a, b, preferred_element_type=f32)


def iota(shape, dim):
    return lax.broadcasted_iota(i32, shape, dim)


def as_bf16(mask):
    return mask.astype(f32).astype(bf16)


def fine_mm(values, pair):
    width = pair.shape[1] // 2
    high, low = two(values)
    both = mm(high, pair)
    return both[:, :width] + (both[:, width:] + mm(low, pair[:, :width]))


def fetch(hbm_refs, vmem_refs, sems):
    copies = [pltpu.make_async_copy(src, dst, sems.at[j])
              for j, (src, dst) in enumerate(zip(hbm_refs, vmem_refs))]
    for copy in copies:
        copy.start()
    return copies


def plan_kernel(count_ref, rterm_hbm, cterm_hbm, rhome_hbm, chome_hbm, traces_hbm,
                pay_ref, slot_hbm, rterm_ref, cterm_ref, rhome_ref, chome_ref, tbuf, slot_ref, sems):
    parts = [pl.ds(j * 128, 128) for j in range(4)]
    copies = fetch([rterm_hbm, cterm_hbm, rhome_hbm, chome_hbm] + [traces_hbm.at[p] for p in parts],
                   [rterm_ref, cterm_ref, rhome_ref, chome_ref] + [tbuf.at[p] for p in parts], sems)
    before_mask = as_bf16(iota((ROWS, ROWS), 0) < iota((ROWS, ROWS), 1))

    def look_up(term, home, bits):
        high, low = term >> 7, term & 127
        owner_t = jnp.transpose((home >> bits).astype(f32)).astype(bf16)
        place_t = jnp.transpose((home & (2 ** bits - 1)).astype(f32)).astype(bf16)
        pick_high = as_bf16(iota((home.shape[0], ROWS), 0) == high)
        pick_low = iota((128, ROWS), 0) == low
        owner = jnp.sum(jnp.where(pick_low, mm(owner_t, pick_high), 0.0), axis=0, keepdims=True)
        place = jnp.sum(jnp.where(pick_low, mm(place_t, pick_high), 0.0), axis=0, keepdims=True)
        mine = iota((DEVS, ROWS), 0) == owner.astype(i32)
        mine16 = as_bf16(mine)
        before = mm(mine16, before_mask)
        rank = jnp.sum(jnp.where(mine, before, 0.0), axis=0, keepdims=True)
        return owner, place, rank, mine16

    for copy in copies[:4]:
        copy.wait()
    r_owner, r_place, r_rank, r_mine = look_up(rterm_ref[...], rhome_ref[...], 7)
    c_owner, c_place, c_rank, c_mine = look_up(cterm_ref[...], chome_ref[...], 8)
    live = (iota((1, ROWS), 1) < count_ref[0]).astype(f32)
    r_slot = r_owner * PAIR + r_rank
    c_slot = c_owner * PAIR + (c_rank + CAP)
    powers = []
    for j in range(4):
        copies[4 + j].wait()
        total = jnp.zeros((128, 128), f32)
        for b in range(BLOCKS):
            x = tbuf[j * 128:(j + 1) * 128, b * 128:(b + 1) * 128].astype(f32)
            total = total + x * x
        powers.append(jnp.sum(jnp.transpose(total), axis=0, keepdims=True))
    power = jnp.concatenate(powers, axis=1) * live
    slot_ref[...] = jnp.concatenate(
        [r_slot, c_slot, live, power, jnp.zeros((4, ROWS), f32)], axis=0)
    save = pltpu.make_async_copy(slot_ref, slot_hbm, sems.at[8])
    save.start()
    p_high, p_low = two(power)
    p_high, p_low = p_high.astype(f32), p_low.astype(f32)
    line = iota((2 * PAIR, ROWS), 0).astype(f32)

    def weights(rank, place):
        at_place = jnp.where(line == rank, place, 0.0)
        here = line == rank + PAIR
        return ((at_place + jnp.where(here, p_high, 0.0)).astype(bf16),
                jnp.where(here, p_low, 0.0).astype(bf16))

    pay = jnp.zeros((DEVS, 2 * PAIR), f32)
    for mine, rank, place in ((r_mine, r_rank, r_place), (c_mine, c_rank + CAP, c_place)):
        for weight in weights(rank, place):
            pay = pay + lax.dot_general(mine, weight, NT, preferred_element_type=f32)
    pay_ref[...] = pay
    save.wait()


def pick_kernel(got_ref, rcv_ref, cmp_ref, out_hbm, out_ref, sem):
    got = got_ref[...].astype(i32)
    rcv_pair = jnp.concatenate(two(rcv_ref[...]), axis=1)
    cmp_pair = jnp.concatenate(two(cmp_ref[...]), axis=1)
    for s in range(PAIR):
        pair = rcv_pair if s < CAP else cmp_pair
        rows = pair.shape[0]
        pick = as_bf16(iota((DEVS, rows), 1) == got[:, s:s + 1])
        both = mm(pick, pair)
        out_ref[pl.ds(s, DEVS, stride=PAIR), :] = both[:, :TAPS] + both[:, TAPS:]
    save = pltpu.make_async_copy(out_ref, out_hbm, sem)
    save.start()
    save.wait()


def lags_kernel(count_ref, after_ref, traces_ref, targets_ref, f_ref, e_ref, i_ref, c_ref, d_ref,
                even_ref, base_ref, last_ref):
    f_high, f_low = f_ref[:WIN, :], f_ref[WIN:, :]
    e_pair = e_ref[...]
    own = jnp.zeros((ROWBLK, WIN), f32)
    cross = jnp.zeros((ROWBLK, WIN), f32)
    for b in range(BLOCKS):
        now = traces_ref[:, b * 128:(b + 1) * 128]
        goal = targets_ref[:, b * 128:(b + 1) * 128]
        u = mm(jnp.concatenate([now, now], axis=1), e_pair)
        v = mm(jnp.concatenate([goal, goal], axis=1), e_pair)
        if b == 0:
            x = u
        else:
            window = traces_ref[:, (b - 1) * 128:(b + 1) * 128]
            x = mm(window, f_high) + mm(window, f_low)
        xr, xi = x[:, :TAPS], x[:, TAPS:]
        ur, ui = u[:, :TAPS], u[:, TAPS:]
        vr, vi = v[:, :TAPS], v[:, TAPS:]
        own = own + jnp.concatenate([xr * ur + xi * ui, xr * ui - xi * ur], axis=1)
        cross = cross + jnp.concatenate([xr * vr + xi * vi, xr * vi - xi * vr], axis=1)
    i_pair = i_ref[...]
    row = iota((ROWBLK, TAPS), 0) + pl.program_id(0) * ROWBLK
    live = row < count_ref[0]
    even_ref[...] = jnp.where(live, fine_mm(fine_mm(own, i_pair), c_ref[...]), 0.0)
    base_ref[...] = jnp.where(live, fine_mm(cross, i_pair), 0.0)
    final = traces_ref[:, (BLOCKS - 1) * 128:]
    last = mm(jnp.concatenate([final, final], axis=1), d_ref[...])
    last_ref[...] = jnp.where(jnp.concatenate([live, live], axis=1), last, 0.0)


def books_kernel(got_ref, slot_ref, srcloc_ref, src_ref,
                 settle_ref, energy_ref, rcol_ref, ccol_ref, line_ref, shot_ref, scale_ref):
    got = jnp.concatenate([got_ref[...], jnp.zeros((DEVS, 128 - 2 * PAIR), f32)], axis=1)
    turned = jnp.transpose(got)[:2 * PAIR]
    first = turned.astype(bf16)
    rest = turned - first.astype(f32)
    second = rest.astype(bf16)
    third = (rest - second.astype(f32)).astype(bf16)
    q = iota((DEVS, SLOTS), 1)
    spread = as_bf16((q >> 4) == iota((DEVS, SLOTS), 0))
    wide = mm(first, spread) + (mm(second, spread) + mm(third, spread))
    line = iota((PAIR, SLOTS), 0)
    slot = iota((PAIR, SLOTS), 1) & (PAIR - 1)
    place = jnp.sum(jnp.where(line == slot, wide[:PAIR], 0.0), axis=0, keepdims=True)
    power = jnp.sum(jnp.where(line == slot, wide[PAIR:], 0.0), axis=0, keepdims=True)
    place = place.astype(i32) + ((iota((1, SLOTS), 1) & CAP) << 4)
    for c in range(3):
        rows = iota((128, SLOTS), 0) + c * 128
        settle_ref[c * 128:(c + 1) * 128, :] = as_bf16(rows == place)
        energy = jnp.sum(jnp.where(rows == place, power, 0.0), axis=1, keepdims=True)
        energy_ref[c * 128:(c + 1) * 128, :] = jnp.broadcast_to(
            step_size / jnp.maximum(energy, 1.0), (128, 128))
    lines = jnp.concatenate(
        [slot_ref[...], srcloc_ref[...].astype(f32), jnp.zeros((128 - 9, ROWS), f32)], axis=0)
    src = src_ref[...]
    for j in range(4):
        part = slice(j * 128, (j + 1) * 128)
        col = jnp.transpose(lines[:, part])
        rcol_ref[part, :] = jnp.broadcast_to(col[:, 0:1].astype(i32), (128, 128)).astype(jnp.int16)
        ccol_ref[part, :] = jnp.broadcast_to(col[:, 1:2].astype(i32), (128, 128)).astype(jnp.int16)
        src_rows = jnp.zeros((128, TAPS), f32)
        for s in range(SRC):
            src_rows = jnp.where(col[:, 8:9] == float(s), src[s:s + 1, :], src_rows)
        shot_ref[part, :] = src_rows
    for j in range(2):
        line_ref[16 * j:16 * (j + 1), :] = jnp.broadcast_to(
            slot_ref[j:j + 1, :].astype(i32), (16, ROWS)).astype(jnp.int16)
    mine = iota((8, ROWS), 0) == srcloc_ref[...]
    energy = jnp.sum(jnp.where(mine, slot_ref[3:4, :], 0.0), axis=1, keepdims=True)
    scale_ref[:8, :] = jnp.broadcast_to(step_size / jnp.maximum(energy, 1.0), (8, TAPS))
    scale_ref[8:, :] = jnp.concatenate([src, jnp.zeros((8 - SRC, TAPS), f32)], axis=0)


def one_hot16(at, first, second):
    ones = jnp.ones(at.shape, bf16)
    return jnp.where((at == first) | (at == second), ones, jnp.zeros(at.shape, bf16))


def grad_kernel(*refs):
    hbm, (out_hbm, src_out_ref) = refs[:13], refs[13:15]
    vmem, out_ref, sems = refs[15:28], refs[28], refs[29]
    chunk = 256
    chunks = SLOTS // chunk
    parts = [pl.ds(k * chunk, chunk) for k in range(chunks)]
    sources = list(hbm[:2]) + [hbm[2].at[p] for p in parts] + list(hbm[3:])
    targets = list(vmem[:2]) + [vmem[2].at[p] for p in parts] + list(vmem[3:])
    copies = fetch(sources, targets, sems)
    (rcol_ref, ccol_ref, fetched_ref, shot_ref, d_ref, last_ref, tail_ref, even_ref, i_ref, base_ref,
     line_ref, srcloc_ref, scale_src_ref) = vmem
    pieces, others = copies[2:2 + chunks], copies[2 + chunks:]
    lane = lax.broadcasted_iota(jnp.int16, (ROWS, 128), 1)
    copies[0].wait()
    copies[1].wait()
    rcol, ccol = rcol_ref[...], ccol_ref[...]
    both = jnp.zeros((ROWS, 2 * TAPS), f32)
    for k in range(chunks):
        pick = jnp.concatenate(
            [one_hot16(lane + jnp.int16(k * chunk + j * 128), rcol, ccol) for j in range(chunk // 128)],
            axis=1)
        pieces[k].wait()
        rows = jnp.concatenate(two(fetched_ref[k * chunk:(k + 1) * chunk, :]), axis=1)
        both = both + mm(pick, rows)
    for copy in others:
        copy.wait()
    mixed = (shot_ref[...] + (both[:, :TAPS] + both[:, TAPS:])).astype(bf16)
    h = mm(jnp.concatenate([mixed, mixed], axis=1), d_ref[...])
    hr, hi = h[:, :TAPS], h[:, TAPS:]
    xr, xi = last_ref[:, :TAPS], last_ref[:, TAPS:]
    past = jnp.concatenate([xr * hr - xi * hi, xr * hi + xi * hr], axis=1)
    m = mm(past.astype(bf16), tail_ref[...])
    mr, mi = m[:, :TAPS], m[:, TAPS:]
    even = even_ref[...]
    spectrum = jnp.concatenate(
        [even * hr - (xr * mr + xi * mi), even * hi - (xr * mi - xi * mr)], axis=1)
    grad = fine_mm(spectrum, i_ref[...]) - base_ref[...]
    rows = jnp.concatenate(two(grad), axis=1)
    first = jnp.concatenate([line_ref[:16, :]] * (chunk // 16), axis=0)
    second = jnp.concatenate([line_ref[16:, :]] * (chunk // 16), axis=0)
    saves = []
    for k in range(chunks):
        at = lax.broadcasted_iota(jnp.int16, (chunk, ROWS), 0) + jnp.int16(k * chunk)
        both = mm(one_hot16(at, first, second), rows)
        out_ref[k * chunk:(k + 1) * chunk, :] = both[:, :TAPS] + both[:, TAPS:]
        saves.append(pltpu.make_async_copy(out_ref.at[parts[k]], out_hbm.at[parts[k]],
                                           sems.at[12 + chunks + k]))
        saves[-1].start()
    mine = as_bf16(iota((8, ROWS), 0) == srcloc_ref[...])
    both = mm(mine, rows)
    src_out_ref[...] = scale_src_ref[8:8 + SRC, :] - ((both[:, :TAPS] + both[:, TAPS:])
                                                      * scale_src_ref[:8, :])[:SRC]
    for save in saves:
        save.wait()


def settle_kernel(grads_ref, pick_ref, energy_ref, rcv_ref, cmp_ref, rcv_out_ref, cmp_out_ref):
    total = jnp.zeros((RCV + CMP, 2 * TAPS), f32)
    width = 512
    for k in range(SLOTS // width):
        rows = jnp.concatenate(two(grads_ref[k * width:(k + 1) * width, :]), axis=1)
        total = total + mm(pick_ref[:, k * width:(k + 1) * width], rows)
    change = (total[:, :TAPS] + total[:, TAPS:]) * energy_ref[...]
    rcv_out_ref[...] = rcv_ref[...] - change[:RCV]
    cmp_out_ref[...] = cmp_ref[...] - change[RCV:]


def shape(*dims, dtype=f32):
    return jax.ShapeDtypeStruct(dims, dtype)


VM = pl.BlockSpec(memory_space=pltpu.VMEM)
SM = pl.BlockSpec(memory_space=pltpu.SMEM)
HB = pl.BlockSpec(memory_space=pltpu.HBM)
DMA = pltpu.SemaphoreType.DMA
small = pltpu.CompilerParams(vmem_limit_bytes=24 * MIB)
large = pltpu.CompilerParams(vmem_limit_bytes=60 * MIB + MIB // 2)


def whole(array):
    return pl.BlockSpec(array.shape, lambda i: (0,) * len(array.shape))


def body(traces, targets, src_local, rcv_term, cmp_term, rcv_home, cmp_home, counts,
         src_filters, rcv_filters, cmp_filters):
    tables = {name: jnp.asarray(value) for name, value in make_tables().items()}
    src_line = src_local.reshape(1, ROWS)
    pay, slot_lines = pl.pallas_call(
        plan_kernel,
        out_shape=(shape(DEVS, 2 * PAIR), shape(8, ROWS)),
        in_specs=[SM, HB, HB, HB, HB, HB],
        out_specs=(VM, HB),
        scratch_shapes=[pltpu.VMEM((1, ROWS), i32), pltpu.VMEM((1, ROWS), i32),
                        pltpu.VMEM((128, 128), i32), pltpu.VMEM((256, 128), i32),
                        pltpu.VMEM((ROWS, NS), bf16), pltpu.VMEM((8, ROWS), f32), DMA((9,))],
        compiler_params=large,
        name="plan",
    )(counts, rcv_term.reshape(1, ROWS), cmp_term.reshape(1, ROWS),
      rcv_home.reshape(-1, 128), cmp_home.reshape(-1, 128), traces)
    got = lax.all_to_all(pay, AXES, split_axis=0, concat_axis=0, tiled=True)
    values = pl.pallas_call(
        pick_kernel,
        out_shape=shape(SLOTS, TAPS),
        in_specs=[VM] * 3, out_specs=HB,
        scratch_shapes=[pltpu.VMEM((SLOTS, TAPS), f32), DMA],
        compiler_params=small,
        name="pick",
    )(got, rcv_filters, cmp_filters)
    fetched = lax.all_to_all(values.reshape(DEVS, PAIR, TAPS), AXES, split_axis=0, concat_axis=0,
                             tiled=True).reshape(SLOTS, TAPS)

    def blk(width):
        return pl.BlockSpec((ROWBLK, width), lambda i: (i, 0))

    even, base, last = pl.pallas_call(
        lags_kernel,
        grid=(ROWS // ROWBLK,),
        out_shape=(shape(ROWS, TAPS), shape(ROWS, TAPS), shape(ROWS, WIN)),
        in_specs=[SM, pl.BlockSpec((8, 2 * PAIR), lambda i: (0, 0)), blk(NS), blk(NS)]
        + [whole(tables[n]) for n in "feicd"],
        out_specs=(blk(TAPS), blk(TAPS), blk(WIN)),
        compiler_params=large,
        cost_estimate=pl.CostEstimate(flops=5 * 10 ** 9, bytes_accessed=5 * 10 ** 6,
                                      transcendentals=0),
        name="lags",
    )(counts, got, traces, targets, *[tables[n] for n in "feicd"])
    int16 = jnp.int16
    book_shapes = (shape(RCV + CMP, SLOTS, dtype=bf16), shape(RCV + CMP, TAPS),
                   shape(ROWS, TAPS, dtype=int16), shape(ROWS, TAPS, dtype=int16),
                   shape(32, ROWS, dtype=int16), shape(ROWS, TAPS), shape(16, TAPS))
    book_in = (got, slot_lines, src_line, src_filters)
    settle_pick, energy, rcol, ccol, lines, shots, scale = pl.pallas_call(
        books_kernel,
        grid=(1,),
        out_shape=book_shapes,
        in_specs=[whole(a) for a in book_in], out_specs=[whole(a) for a in book_shapes],
        compiler_params=large,
        name="books",
    )(*book_in)
    held = (rcol, ccol, fetched, shots, tables["d"], last, tables["tail"], even, tables["i"], base,
            lines, src_line, scale)
    send, src_out = pl.pallas_call(
        grad_kernel,
        out_shape=(shape(SLOTS, TAPS), shape(SRC, TAPS)),
        in_specs=[HB] * len(held), out_specs=(HB, VM),
        scratch_shapes=[pltpu.VMEM(a.shape, a.dtype) for a in held]
        + [pltpu.VMEM((SLOTS, TAPS), f32), DMA((28,))],
        compiler_params=large,
        name="grad",
    )(*held)
    back = lax.all_to_all(send.reshape(DEVS, PAIR, TAPS), AXES, split_axis=0, concat_axis=0,
                          tiled=True).reshape(SLOTS, TAPS)
    rcv_out, cmp_out = pl.pallas_call(
        settle_kernel,
        out_shape=(shape(RCV, TAPS), shape(CMP, TAPS)),
        in_specs=[VM] * 5, out_specs=(VM, VM),
        compiler_params=small,
        name="settle",
    )(back, settle_pick, energy, rcv_filters, cmp_filters)
    return src_out, rcv_out, cmp_out


def solution(mesh):
    rows = P(AXES, None)
    flat = P(AXES)
    return jax.shard_map(
        body,
        mesh=mesh,
        in_specs=(rows, rows, flat, flat, flat, P(), P(), flat, rows, rows, rows),
        out_specs=(rows, rows, rows),
        check_vma=False,
    )
```

time: 95.3 us -> 83.8 us (0.88)
  local copies, waits for them, and re-layouts: 21.8 us -> 1 us
  Pallas kernels: 17.1 us -> 25.2 us
  waiting for transfers between devices: 1.47 us -> 6.93 us
  blocking collectives: 48.5 us -> 44.7 us
    unnamed x62 -> x12, local copies, waits for them, and re-layouts: 21.8 us -> 1 us
    all_to_all x1, waiting for transfers between devices: 1.47 us -> 6.93 us  [body(): lax.all_to_all(values.reshape(DEVS, PAIR, TAPS), AXES, split_axis=0, conc...]
    all_to_all x1, blocking collectives: 27.6 us -> 23.6 us  [body(): lax.all_to_all(send.reshape(DEVS, PAIR, TAPS), AXES, split_axis=0, concat...]
    pallas_call x1, Pallas kernels: 0.92 us -> 3.43 us  [body(): pl.pallas_call(books_kernel, grid=(1,), out_shape=book_shapes, in_specs=[...]
    pallas_call x1, Pallas kernels: 3.52 us -> 5.78 us  [body(): pl.pallas_call(grad_kernel, out_shape=(shape(SLOTS, TAPS), shape(SRC, TAP...]
    pallas_call x1, Pallas kernels: 6.99 us -> 9.15 us  [body(): pl.pallas_call(lags_kernel, grid=(ROWS // ROWBLK,), out_shape=(shape(ROWS...]
    pallas_call x1, Pallas kernels: 2.07 us -> 4.03 us  [body(): pl.pallas_call(plan_kernel, out_shape=(shape(DEVS, 2 * PAIR), shape(8, RO...]
  transfers between devices with their start and end apart: 1 -> 1, of which waited for: 1 -> 1; matrix products, arithmetic and copies ran while one was open for 0% -> 0% of each run, Pallas kernels for 8% -> 15%
where the time goes in v2:
time: 83.8 us; the launch traced here: 83.5 us
  blocking collectives  44.7 us (53%)
  Pallas kernels  25.2 us (30%)
  waiting for transfers between devices  6.93 us (8%)
  starting transfers between devices  4.21 us (5%)
  between operations  1.38 us (2%)
  local copies, waits for them, and re-layouts  1 us (1%)
    all_to_all x1, blocking collectives, body(): lax.all_to_all(send.reshape(DEVS, PAIR, TAPS), AXES, split_axis=0, concat...  23.6 us
    all_to_all x1, blocking collectives, body(): got = lax.all_to_all(pay, AXES, split_axis=0, concat_axis=0, tiled=True)  21.1 us
    pallas_call x1, Pallas kernels, body(): pl.pallas_call(lags_kernel, grid=(ROWS // ROWBLK,), out_shape=(shape(ROWS...  9.15 us
    all_to_all x1, waiting for transfers between devices, body(): lax.all_to_all(values.reshape(DEVS, PAIR, TAPS), AXES, split_axis=0, conc...  6.93 us
    pallas_call x1, Pallas kernels, body(): pl.pallas_call(grad_kernel, out_shape=(shape(SLOTS, TAPS), shape(SRC, TAP...  5.78 us
    all_to_all x1, starting transfers between devices, body(): lax.all_to_all(values.reshape(DEVS, PAIR, TAPS), AXES, split_axis=0, conc...  4.21 us
    pallas_call x1, Pallas kernels, body(): pl.pallas_call(plan_kernel, out_shape=(shape(DEVS, 2 * PAIR), shape(8, RO...  4.03 us
    pallas_call x1, Pallas kernels, body(): pl.pallas_call(books_kernel, grid=(1,), out_shape=book_shapes, in_specs=[...  3.43 us
  transfers between devices with their start and end apart: 1, of which 1 were waited for; matrix products, arithmetic and copies ran while one was open for 0% of the time, Pallas kernels for 15%

profile of v2, /device:TPU:1, one launch (start us, length us, event | category | flops | bytes accessed | tf_op | source)
XLA Modules:
  0.0 83.5 jit_solution(8287610799099539398)
XLA Ops:
  0.6 0.0 copy-start.2
  0.6 0.0 copy-start.3
  1.3 4.0 %plan.1 = (f32[128,32]{1,0:T(8,128)}, f32[8,512]{1,0:T(8,128)}) custom-call(s32[1]{0:T(128)S(6)} %copy.21.count_ref, s32[1,512]{1,0:T(1,128)} %bitcast.24, s32[1,512]{1,0:T(1,128)} %bitcast.25, s32[128,128]{1,0:T(8,128)} %bitcast.20, s32[256,128]{1,0:T(8,128)} %bitcast.19, bf16[512,2048]{1,0:T(8,128)(2,1)} %traces_ref.1), custom_call_target="tpu_custom_call" | custom-call | tf_op jit(solution)/shard_map/plan/pallas_call | solution.py:328
  5.4 21.1 %all_to_all.21 = f32[128,1,32]{2,1,0:T(1,128)S(1)} all-to-all(f32[128,1,32]{2,1,0:T(1,128)} %bitcast.21), channel_id=1, replica_groups=mesh['shot'=32,'line'=4] {'shot','line'}, dimensions={0} | all-to-all | bytes 32768 | tf_op jit(solution)/shard_map/all_to_all | solution.py:340
  26.5 0.0 copy-start.1
  26.5 0.0 copy-done.2
  26.5 0.0 copy-done.3
  26.5 1.6 %pick.1 = f32[2048,128]{1,0:T(8,128)} custom-call(f32[128,32]{1,0:T(8,128)S(1)} %bitcast.14, f32[128,128]{1,0:T(8,128)S(1)} %copy-done.3, f32[256,128]{1,0:T(8,128)S(1)} %copy-done.2), custom_call_target="tpu_custom_call" | custom-call | tf_op jit(solution)/shard_map/pick/pallas_call | solution.py:341
  28.1 4.2 %all-to-all-start.1 = ((f32[128,16,128]{2,1,0:T(8,128)}), f32[128,16,128]{2,1,0:T(8,128)S(1)}, u32[]{:S(2)}, u32[]{:S(2)}) async-start(f32[128,16,128]{2,1,0:T(8,128)} %bitcast.8), calls=%async_computation.1 | async-start | bytes 2097152 | tf_op jit(solution)/shard_map/all_to_all | solution.py:349
  32.3 0.0 copy-done.1
  32.3 3.4 %books.1 = (bf16[384,2048]{1,0:T(8,128)(2,1)}, f32[384,128]{1,0:T(8,128)}, s16[512,128]{1,0:T(8,128)(2,1)}, s16[512,128]{1,0:T(8,128)(2,1)}, s16[32,512]{1,0:T(8...) custom-call(f32[128,32]{1,0:T(8,128)} %bitcast.15, f32[8,512]{1,0:T(8,128)} %get-tuple-element.20.slot_ref, ...), custom_call_target="tpu_custom_call" | custom-call | tf_op jit(solution)/shard_map/books/pallas_call | solution.py:372
  35.7 9.2 %lags.1 = (f32[512,128]{1,0:T(8,128)}, f32[512,128]{1,0:T(8,128)}, f32[512,256]{1,0:T(8,128)}) custom-call(s32[1]{0:T(128)S(6)} %copy.21.count_ref, f32[128,32]{1,0:T(8,128)} %bitcast.16, bf16[512,2048]{1,0:T(8,128)(2,1)} %traces_ref.1, bf16[512,2048]{1,0:T(8,128)(2,1)} %targets_ref.1, bf16[512,256]{1,0:T(8,128)(2,1)} %constant.12.clone.f_ref, ...), custom_call_target="tpu_custom_call" | custom-call | flops 5000000000 | bytes 5000000 | tf_op jit(solution)/shard_map/lags/pallas_call | solution.py:355
  44.9 6.9 %all-to-all-done.1 = f32[128,16,128]{2,1,0:T(8,128)S(1)} async-done(((f32[128,16,128]{2,1,0:T(8,128)}), f32[128,16,128]{2,1,0:T(8,128)S(1)}, u32[]{:S(2)}, u32[]{:S(2)}) %all-to-all-start.1) | async-done | bytes 1048608 | tf_op jit(solution)/shard_map/all_to_all | solution.py:349
  51.8 0.0 copy-start.5
  51.8 1.0 %copy-done.5 = f32[128,16,128]{2,1,0:T(8,128)} copy-done((f32[128,16,128]{2,1,0:T(8,128)}, f32[128,16,128]{2,1,0:T(8,128)S(1)}, u32[]{:S(2)}) %copy-start.5) | copy-done | bytes 1048600
  52.8 0.0 copy-start
  52.8 0.0 copy-start.4
  52.8 5.8 %grad.1 = (f32[2048,128]{1,0:T(8,128)}, f32[4,128]{1,0:T(4,128)}) custom-call(s16[512,128]{1,0:T(8,128)(2,1)} %get-tuple-element.21.refs_0_, s16[512,128]{1,0:T(8,128)(2,1)} %get-tuple-element.22.refs_1_, f32[2048,128]{1,0:T(8,128)} %bitcast.17, f32[512,128]{1,0:T(8,128)} %get-tuple-element.23.refs_3_, bf16[256,256]{1,0:T(8,128)(2,1)} %constant.13.clone.d_ref.refs_4_, ...), custom_call_target="tpu_custom_call" | custom-call | tf_op jit(solution)/shard_map/grad/pallas_call | solution.py:382
  58.6 23.6 %all_to_all.22 = f32[128,16,128]{2,1,0:T(8,128)S(1)} all-to-all(f32[128,16,128]{2,1,0:T(8,128)} %bitcast.18), channel_id=1, replica_groups=mesh['shot'=32,'line'=4] {'shot','line'}, dimensions={0} | all-to-all | bytes 2097152 | tf_op jit(solution)/shard_map/all_to_all | solution.py:391
  82.2 0.0 copy-done
  82.2 0.0 copy-done.4
  82.2 1.2 %settle.1 = (f32[128,128]{1,0:T(8,128)}, f32[256,128]{1,0:T(8,128)}) custom-call(f32[2048,128]{1,0:T(8,128)S(1)} %bitcast.13, bf16[384,2048]{1,0:T(8,128)(2,1)S(1)} %copy-done, f32[384,128]{1,0:T(8,128)S(1)} %copy-done.4, f32[128,128]{1,0:T(8,128)S(1)} %copy-done.3, f32[256,128]{1,0:T(8,128)S(1)} %copy-done.2), custom_call_target="tpu_custom_call" | custom-call | tf_op jit(solution)/shard_map/settle/pallas_call | solution.py:393
Async XLA Ops:
  0.6 25.8 %copy-start.2 = (f32[256,128]{1,0:T(8,128)S(1)}, f32[256,128]{1,0:T(8,128)}, u32[]{:S(2)}) copy-start(f32[256,128]{1,0:T(8,128)} %cmp_ref.3) | copy-start | bytes 393220
  0.6 25.8 %copy-start.3 = (f32[128,128]{1,0:T(8,128)S(1)}, f32[128,128]{1,0:T(8,128)}, u32[]{:S(2)}) copy-start(f32[128,128]{1,0:T(8,128)} %rcv_ref.3) | copy-start | bytes 196612
  26.5 5.9 %copy-start.1 = (f32[128,1,32]{2,1,0:T(1,128)}, f32[128,1,32]{2,1,0:T(1,128)S(1)}, u32[]{:S(2)}) copy-start(f32[128,1,32]{2,1,0:T(1,128)S(1)} %all_to_all.21) | copy-start | bytes 49156
  28.1 23.7 %all-to-all-start.1 = ((f32[128,16,128]{2,1,0:T(8,128)}), f32[128,16,128]{2,1,0:T(8,128)S(1)}, u32[]{:S(2)}, u32[]{:S(2)}) async-start(f32[128,16,128]{2,1,0:T(8,128)} %bitcast.8), calls=%async_computation.1 | async-start | bytes 2097152 | tf_op jit(solution)/shard_map/all_to_all | solution.py:349
  51.8 1.0 %copy-start.5 = (f32[128,16,128]{2,1,0:T(8,128)}, f32[128,16,128]{2,1,0:T(8,128)S(1)}, u32[]{:S(2)}) copy-start(f32[128,16,128]{2,1,0:T(8,128)S(1)} %all-to-all-done.1) | copy-start | bytes 3145732
  52.8 29.4 %copy-start = (bf16[384,2048]{1,0:T(8,128)(2,1)S(1)}, bf16[384,2048]{1,0:T(8,128)(2,1)}, u32[]{:S(2)}) copy-start(bf16[384,2048]{1,0:T(8,128)(2,1)} %get-tuple-element.31.pick_ref) | copy-start | bytes 4718596
  52.8 29.4 %copy-start.4 = (f32[384,128]{1,0:T(8,128)S(1)}, f32[384,128]{1,0:T(8,128)}, u32[]{:S(2)}) copy-start(f32[384,128]{1,0:T(8,128)} %get-tuple-element.32.energy_ref) | copy-start | bytes 589828

commit v3 on v2

v3 whole, which is shorter than its diff:
```python
import jax
import jax.numpy as jnp
import numpy as np
import ml_dtypes
from jax import lax
from jax.experimental import pallas as pl
from jax.experimental.pallas import tpu as pltpu
from jax.sharding import PartitionSpec as P

AXES = ("shot", "line")
DEVS = 128
ROWS = 512
NS = 2048
TAPS = 128
CAP = 8
PAIR = 2 * CAP
SLOTS = DEVS * PAIR
RCV = 128
CMP = 256
SRC = 4
WIN = 256
BLOCKS = NS // TAPS
ROWBLK = 128
step_size = 0.5
f32, bf16, i32 = jnp.float32, jnp.bfloat16, jnp.int32
NT = (((1,), (1,)), ((), ()))
MIB = 1024 * 1024


def split_pair(matrix):
    high = matrix.astype(ml_dtypes.bfloat16)
    low = (matrix - high.astype(np.float64)).astype(ml_dtypes.bfloat16)
    return high, low


def make_tables():
    angle = 2.0 * np.pi * (np.arange(TAPS) + 0.5) / WIN
    place = np.arange(WIN)
    phase = place[:, None] * angle[None, :]
    forward = np.concatenate([np.cos(phase), -np.sin(phase)], axis=1)
    inverse = forward.T / TAPS
    lag_phase = np.arange(TAPS)[:, None] * angle[None, :]
    even = 2.0 * np.cos(lag_phase)
    even[0] = 1.0
    f_high, f_low = split_pair(forward)
    d_pair = np.concatenate(split_pair(forward[:TAPS]), axis=0)
    e_pair = np.concatenate(split_pair(forward[TAPS:]), axis=0)
    i_pair = np.concatenate(split_pair(inverse[:, :TAPS]), axis=1)
    c_pair = np.concatenate(split_pair(even), axis=1)
    tail = split_pair(inverse[:, TAPS:] @ forward[TAPS:])[0]
    f_pair = np.concatenate([f_high, f_low], axis=0)
    return dict(f=f_pair, d=d_pair, e=e_pair, i=i_pair, c=c_pair, tail=tail)


def two(values):
    high = values.astype(bf16)
    low = (values - high.astype(f32)).astype(bf16)
    return high, low


def mm(a, b):
    return jnp.dot(a, b, preferred_element_type=f32)


def iota(shape, dim):
    return lax.broadcasted_iota(i32, shape, dim)


def as_bf16(mask):
    return mask.astype(f32).astype(bf16)


def fine_mm(values, pair):
    width = pair.shape[1] // 2
    high, low = two(values)
    both = mm(high, pair)
    return both[:, :width] + (both[:, width:] + mm(low, pair[:, :width]))


def fetch(hbm_refs, vmem_refs, sems):
    copies = [pltpu.make_async_copy(src, dst, sems.at[j])
              for j, (src, dst) in enumerate(zip(hbm_refs, vmem_refs))]
    for copy in copies:
        copy.start()
    return copies


def flag16(mask):
    return jnp.where(mask, jnp.ones(mask.shape, bf16), jnp.zeros(mask.shape, bf16))


def iota16(shape, dim):
    return lax.broadcasted_iota(jnp.int16, shape, dim)


def row16(row, count):
    tile = jnp.broadcast_to(row.astype(i32), (16, row.shape[1])).astype(jnp.int16)
    return jnp.concatenate([tile] * (count // 16), axis=0)


def plan_kernel(count_ref, rterm_hbm, cterm_hbm, rhome_hbm, chome_hbm, traces_hbm, pay_ref, slot_ref,
                rterm_ref, cterm_ref, rhome_ref, chome_ref, tbuf, sems):
    parts = [pl.ds(j * 128, 128) for j in range(4)]
    copies = fetch(
        [rterm_hbm, cterm_hbm, rhome_hbm, chome_hbm] + [traces_hbm.at[p] for p in parts],
        [rterm_ref, cterm_ref, rhome_ref, chome_ref] + [tbuf.at[p] for p in parts], sems)
    earlier = flag16(iota16((128, 128), 0) < iota16((128, 128), 1))
    count_up = jnp.concatenate([earlier, jnp.ones((128, 128), bf16)], axis=1)

    def look_up(term, home, bits):
        high, low = term >> 7, term & 127
        halves = jnp.concatenate([jnp.transpose((home >> bits).astype(f32)),
                                  jnp.transpose((home & (2 ** bits - 1)).astype(f32))], axis=0)
        rows = home.shape[0]
        both = mm(halves.astype(bf16), flag16(iota16((rows, ROWS), 0) == row16(high, rows)))
        pick_low = iota((128, ROWS), 0) == low
        return (jnp.sum(jnp.where(pick_low, both[:128], 0.0), axis=0, keepdims=True),
                jnp.sum(jnp.where(pick_low, both[128:], 0.0), axis=0, keepdims=True))

    for copy in copies[:4]:
        copy.wait()
    r_owner, r_place = look_up(rterm_ref[...], rhome_ref[...], 7)
    c_owner, c_place = look_up(cterm_ref[...], chome_ref[...], 8)
    for copy in copies[4:]:
        copy.wait()
    line128 = iota16((DEVS, ROWS), 0)
    mine16 = [flag16(line128 == row16(owner, DEVS)) for owner in (r_owner, c_owner)]
    mine = jnp.concatenate(mine16, axis=0)
    owners = jnp.concatenate(
        [jnp.broadcast_to(r_owner, (DEVS, ROWS)), jnp.broadcast_to(c_owner, (DEVS, ROWS))], axis=0)
    here = owners == (iota((2 * DEVS, ROWS), 0) & (DEVS - 1)).astype(f32)
    past = jnp.zeros((2 * DEVS, 128), f32)
    ranks, powers = [], []
    for j in range(4):
        part = slice(j * 128, (j + 1) * 128)
        seen = mm(mine[:, part], count_up)
        before = jnp.where(here[:, part], seen[:, :128] + past, 0.0)
        past = past + seen[:, 128:]
        ranks.append(jnp.concatenate([jnp.sum(before[:DEVS], axis=0, keepdims=True),
                                      jnp.sum(before[DEVS:], axis=0, keepdims=True)], axis=0))
        total = jnp.zeros((128, 128), f32)
        for b in range(BLOCKS):
            x = tbuf[part, b * 128:(b + 1) * 128].astype(f32)
            total = total + x * x
        powers.append(jnp.sum(jnp.transpose(total), axis=0, keepdims=True))
    rank = jnp.concatenate(ranks, axis=1)
    r_rank, c_rank = rank[0:1], rank[1:2] + CAP
    live = (iota((1, ROWS), 1) < count_ref[0]).astype(f32)
    power = jnp.concatenate(powers, axis=1) * live
    slot_ref[...] = jnp.concatenate(
        [r_owner * PAIR + r_rank, c_owner * PAIR + c_rank, live, power, jnp.zeros((4, ROWS), f32)],
        axis=0)
    p_high = power.astype(bf16).astype(f32)
    p_low = power - p_high
    line = iota((PAIR, ROWS), 0).astype(f32)

    def weights(rank, place):
        at = line == rank
        return jnp.concatenate(
            [jnp.where(at, row, 0.0) for row in (place, p_high, p_low)], axis=0).astype(bf16)

    pay_ref[...] = lax.dot_general(
        jnp.concatenate(mine16, axis=1),
        jnp.concatenate([weights(r_rank, r_place), weights(c_rank, c_place)], axis=1),
        NT, preferred_element_type=f32)


def pick_kernel(got_ref, rcv_ref, cmp_ref, out_hbm, out_ref, sems):
    pairs = [jnp.concatenate(two(t[...]), axis=1) for t in (rcv_ref, cmp_ref)]
    half = DEVS // 2
    saves = []
    for h in range(2):
        got = got_ref[h * half:(h + 1) * half, :PAIR].astype(i32)
        for side, pair in enumerate(pairs):
            lane = iota((half, pair.shape[0]), 1)
            pick = jnp.concatenate(
                [as_bf16(lane == got[:, s:s + 1]) for s in range(side * CAP, (side + 1) * CAP)], axis=0)
            both = mm(pick, pair)
            values = both[:, :TAPS] + both[:, TAPS:]
            for s in range(CAP):
                out_ref[pl.ds(h * half * PAIR + side * CAP + s, half, stride=PAIR), :] = (
                    values[s * half:(s + 1) * half])
        part = pl.ds(h * half * PAIR, half * PAIR)
        saves.append(pltpu.make_async_copy(out_ref.at[part], out_hbm.at[part], sems.at[h]))
        saves[-1].start()
    for save in saves:
        save.wait()


def lags_kernel(after_ref, traces_ref, targets_ref, f_ref, e_ref, i_ref, c_ref, d_ref,
                even_ref, base_ref, last_ref):
    f_high, f_low = f_ref[:WIN, :], f_ref[WIN:, :]
    e_pair = e_ref[...]
    own = jnp.zeros((ROWBLK, WIN), f32)
    cross = jnp.zeros((ROWBLK, WIN), f32)
    for b in range(BLOCKS):
        now = traces_ref[:, b * 128:(b + 1) * 128]
        goal = targets_ref[:, b * 128:(b + 1) * 128]
        u = mm(jnp.concatenate([now, now], axis=1), e_pair)
        v = mm(jnp.concatenate([goal, goal], axis=1), e_pair)
        if b == 0:
            x = u
        else:
            window = traces_ref[:, (b - 1) * 128:(b + 1) * 128]
            x = mm(window, f_high) + mm(window, f_low)
        xr, xi = x[:, :TAPS], x[:, TAPS:]
        ur, ui = u[:, :TAPS], u[:, TAPS:]
        vr, vi = v[:, :TAPS], v[:, TAPS:]
        own = own + jnp.concatenate([xr * ur + xi * ui, xr * ui - xi * ur], axis=1)
        cross = cross + jnp.concatenate([xr * vr + xi * vi, xr * vi - xi * vr], axis=1)
    i_pair = i_ref[...]
    even_ref[...] = fine_mm(fine_mm(own, i_pair), c_ref[...])
    base_ref[...] = fine_mm(cross, i_pair)
    final = traces_ref[:, (BLOCKS - 1) * 128:]
    last_ref[...] = mm(jnp.concatenate([final, final], axis=1), d_ref[...])


def books_kernel(got_ref, slot_ref, srcloc_ref, src_ref,
                 settle_ref, energy_ref, rcol_ref, ccol_ref, line_ref, shot_ref, scale_ref):
    got = jnp.concatenate([got_ref[...], jnp.zeros((DEVS, 128 - 3 * PAIR), f32)], axis=1)
    turned = jnp.transpose(got)[:3 * PAIR].astype(bf16)
    q = iota((DEVS, SLOTS), 1)
    spread = as_bf16((q >> 4) == iota((DEVS, SLOTS), 0))
    wide = mm(turned, spread)
    line = iota((PAIR, SLOTS), 0)
    slot = iota((PAIR, SLOTS), 1) & (PAIR - 1)
    place = jnp.sum(jnp.where(line == slot, wide[:PAIR], 0.0), axis=0, keepdims=True)
    power = jnp.sum(jnp.where(line == slot, wide[PAIR:2 * PAIR] + wide[2 * PAIR:], 0.0), axis=0, keepdims=True)
    place = place.astype(i32) + ((iota((1, SLOTS), 1) & CAP) << 4)
    for c in range(3):
        rows = iota((128, SLOTS), 0) + c * 128
        settle_ref[c * 128:(c + 1) * 128, :] = as_bf16(rows == place)
        energy = jnp.sum(jnp.where(rows == place, power, 0.0), axis=1, keepdims=True)
        energy_ref[c * 128:(c + 1) * 128, :] = jnp.broadcast_to(
            step_size / jnp.maximum(energy, 1.0), (128, 128))
    lines = jnp.concatenate(
        [slot_ref[...], srcloc_ref[...].astype(f32), jnp.zeros((128 - 9, ROWS), f32)], axis=0)
    src = src_ref[...]
    for j in range(4):
        part = slice(j * 128, (j + 1) * 128)
        col = jnp.transpose(lines[:, part])
        rcol_ref[part, :] = jnp.broadcast_to(col[:, 0:1].astype(i32), (128, 128)).astype(jnp.int16)
        ccol_ref[part, :] = jnp.broadcast_to(col[:, 1:2].astype(i32), (128, 128)).astype(jnp.int16)
        src_rows = jnp.zeros((128, TAPS), f32)
        for s in range(SRC):
            src_rows = jnp.where(col[:, 8:9] == float(s), src[s:s + 1, :], src_rows)
        shot_ref[part, :] = src_rows
    live = slot_ref[2:3, :] > 0.0
    for j, row in enumerate((slot_ref[0:1, :], slot_ref[1:2, :], srcloc_ref[...].astype(f32))):
        line_ref[16 * j:16 * (j + 1), :] = jnp.broadcast_to(
            jnp.where(live, row, -1.0).astype(i32), (16, ROWS)).astype(jnp.int16)
    mine = iota((8, ROWS), 0) == srcloc_ref[...]
    energy = jnp.sum(jnp.where(mine, slot_ref[3:4, :], 0.0), axis=1, keepdims=True)
    scale_ref[:8, :] = jnp.broadcast_to(step_size / jnp.maximum(energy, 1.0), (8, TAPS))
    scale_ref[8:, :] = jnp.concatenate([src, jnp.zeros((8 - SRC, TAPS), f32)], axis=0)


def one_hot16(at, first, second):
    ones = jnp.ones(at.shape, bf16)
    return jnp.where((at == first) | (at == second), ones, jnp.zeros(at.shape, bf16))


def grad_kernel(fetched_ref, *refs):
    hbm_refs, (out_ref, src_out_ref) = refs[:11], refs[11:13]
    vmem_refs, sems = refs[13:24], refs[24]
    copies = fetch(hbm_refs, vmem_refs, sems)
    (rcol_ref, ccol_ref, shot_ref, d_ref, even_ref, last_ref, tail_ref, i_ref, base_ref,
     line_ref, scale_ref) = vmem_refs
    chunk = 512
    chunks = SLOTS // chunk
    lane = iota16((ROWS, 128), 1)
    first_rows = jnp.concatenate(two(fetched_ref[:chunk, :]), axis=1)
    for copy in copies[:2]:
        copy.wait()
    rcol, ccol = rcol_ref[...], ccol_ref[...]
    both = None
    for k in range(chunks):
        pick = jnp.concatenate(
            [one_hot16(lane + jnp.int16(k * chunk + j * 128), rcol, ccol) for j in range(chunk // 128)],
            axis=1)
        if k == 0:
            both = mm(pick, first_rows)
        else:
            rows = jnp.concatenate(two(fetched_ref[k * chunk:(k + 1) * chunk, :]), axis=1)
            both = both + mm(pick, rows)
    for copy in copies[2:]:
        copy.wait()
    mixed = (shot_ref[...] + (both[:, :TAPS] + both[:, TAPS:])).astype(bf16)
    h = mm(jnp.concatenate([mixed, mixed], axis=1), d_ref[...])
    hr, hi = h[:, :TAPS], h[:, TAPS:]
    xr, xi = last_ref[:, :TAPS], last_ref[:, TAPS:]
    past = jnp.concatenate([xr * hr - xi * hi, xr * hi + xi * hr], axis=1)
    m = mm(past.astype(bf16), tail_ref[...])
    mr, mi = m[:, :TAPS], m[:, TAPS:]
    even = even_ref[...]
    spectrum = jnp.concatenate(
        [even * hr - (xr * mr + xi * mi), even * hi - (xr * mi - xi * mr)], axis=1)
    grad = fine_mm(spectrum, i_ref[...]) - base_ref[...]
    rows = jnp.concatenate(two(grad), axis=1)
    first = jnp.concatenate([line_ref[:16, :]] * (chunk // 16), axis=0)
    second = jnp.concatenate([line_ref[16:32, :]] * (chunk // 16), axis=0)
    for k in range(chunks):
        at = iota16((chunk, ROWS), 0) + jnp.int16(k * chunk)
        both = mm(one_hot16(at, first, second), rows)
        out_ref[k * chunk:(k + 1) * chunk, :] = both[:, :TAPS] + both[:, TAPS:]
    both = mm(flag16(iota16((16, ROWS), 0) == line_ref[32:, :]), rows)
    src_out_ref[...] = scale_ref[8:8 + SRC, :] - ((both[:8, :TAPS] + both[:8, TAPS:])
                                                  * scale_ref[:8, :])[:SRC]


def settle_kernel(grads_ref, pick_ref, energy_ref, rcv_ref, cmp_ref, rcv_out_ref, cmp_out_ref):
    total = jnp.zeros((RCV + CMP, 2 * TAPS), f32)
    width = 512
    for k in range(SLOTS // width):
        rows = jnp.concatenate(two(grads_ref[k * width:(k + 1) * width, :]), axis=1)
        total = total + mm(pick_ref[:, k * width:(k + 1) * width], rows)
    change = (total[:, :TAPS] + total[:, TAPS:]) * energy_ref[...]
    rcv_out_ref[...] = rcv_ref[...] - change[:RCV]
    cmp_out_ref[...] = cmp_ref[...] - change[RCV:]


def shape(*dims, dtype=f32):
    return jax.ShapeDtypeStruct(dims, dtype)


VM = pl.BlockSpec(memory_space=pltpu.VMEM)
HB = pl.BlockSpec(memory_space=pltpu.HBM)
DMA = pltpu.SemaphoreType.DMA
small = pltpu.CompilerParams(vmem_limit_bytes=24 * MIB)
large = pltpu.CompilerParams(vmem_limit_bytes=60 * MIB + MIB // 2)


def whole(array):
    return pl.BlockSpec(array.shape, lambda i: (0,) * len(array.shape))


def in_hbm(*arrays):
    return [pltpu.with_memory_space_constraint(a, pltpu.HBM) for a in arrays]


def hbm(*dims, dtype=f32):
    return pltpu.HBM(dims, dtype)


def vmem(*dims, dtype=f32):
    return pltpu.VMEM(dims, dtype)


def run_plan(traces, rcv_term, cmp_term, rcv_home, cmp_home, counts):
    args = in_hbm(rcv_term.reshape(1, ROWS), cmp_term.reshape(1, ROWS),
                  rcv_home.reshape(-1, 128), cmp_home.reshape(-1, 128), traces)
    return pl.pallas_call(
        plan_kernel,
        out_shape=(vmem(DEVS, 3 * PAIR), vmem(8, ROWS)),
        in_specs=[pl.BlockSpec(memory_space=pltpu.SMEM)] + [HB] * 5,
        out_specs=(VM, VM),
        scratch_shapes=[vmem(1, ROWS, dtype=i32), vmem(1, ROWS, dtype=i32),
                        vmem(128, 128, dtype=i32), vmem(256, 128, dtype=i32),
                        vmem(ROWS, NS, dtype=bf16), DMA((8,))],
        compiler_params=small,
        name="plan",
    )(counts, *args)


def run_pick(got, rcv_filters, cmp_filters):
    return pl.pallas_call(
        pick_kernel,
        out_shape=hbm(SLOTS, TAPS),
        in_specs=[VM] * 3, out_specs=HB,
        scratch_shapes=[vmem(SLOTS, TAPS), DMA((2,))],
        compiler_params=small,
        name="pick",
    )(got, rcv_filters, cmp_filters)


def run_lags(got, traces, targets, tables):
    def blk(width):
        return pl.BlockSpec((ROWBLK, width), lambda i: (i, 0))

    return pl.pallas_call(
        lags_kernel,
        grid=(ROWS // ROWBLK,),
        out_shape=(hbm(ROWS, TAPS), hbm(ROWS, TAPS), hbm(ROWS, WIN)),
        in_specs=[pl.BlockSpec((8, 3 * PAIR), lambda i: (0, 0)), blk(NS), blk(NS)]
        + [whole(tables[n]) for n in "feicd"],
        out_specs=(blk(TAPS), blk(TAPS), blk(WIN)),
        compiler_params=large,
        cost_estimate=pl.CostEstimate(flops=5 * 10 ** 9, bytes_accessed=5 * 10 ** 6,
                                      transcendentals=0),
        name="lags",
    )(*in_hbm(got, traces, targets, *[tables[n] for n in "feicd"]))


def run_books(got, slot_lines, src_line, src_filters):
    int16 = jnp.int16
    out = (hbm(RCV + CMP, SLOTS, dtype=bf16), hbm(RCV + CMP, TAPS),
           hbm(ROWS, TAPS, dtype=int16), hbm(ROWS, TAPS, dtype=int16),
           hbm(48, ROWS, dtype=int16), hbm(ROWS, TAPS), hbm(16, TAPS))
    args = (got, slot_lines, src_line, src_filters)
    return pl.pallas_call(
        books_kernel,
        grid=(1,),
        out_shape=out,
        in_specs=[whole(a) for a in args], out_specs=[whole(a) for a in out],
        compiler_params=large,
        name="books",
    )(got, slot_lines, *in_hbm(*args[2:]))


def run_grad(fetched, held):
    return pl.pallas_call(
        grad_kernel,
        out_shape=(vmem(SLOTS, TAPS), vmem(SRC, TAPS)),
        in_specs=[VM] + [HB] * len(held), out_specs=(VM, VM),
        scratch_shapes=[vmem(*a.shape, dtype=a.dtype) for a in held] + [DMA((len(held),))],
        compiler_params=small,
        name="grad",
    )(pltpu.with_memory_space_constraint(fetched, pltpu.VMEM), *in_hbm(*held))


def run_settle(back, settle_pick, energy, rcv_filters, cmp_filters):
    return pl.pallas_call(
        settle_kernel,
        out_shape=(shape(RCV, TAPS), shape(CMP, TAPS)),
        in_specs=[VM] * 5, out_specs=(VM, VM),
        compiler_params=small,
        name="settle",
    )(back, settle_pick, energy, rcv_filters, cmp_filters)


def swap(rows):
    return lax.all_to_all(rows.reshape(DEVS, PAIR, TAPS), AXES, split_axis=0, concat_axis=0,
                          tiled=True).reshape(SLOTS, TAPS)


def body(traces, targets, src_local, rcv_term, cmp_term, rcv_home, cmp_home, counts,
         src_filters, rcv_filters, cmp_filters):
    tables = {name: jnp.asarray(value) for name, value in make_tables().items()}
    src_line = src_local.reshape(1, ROWS)
    pay, slot_lines = run_plan(traces, rcv_term, cmp_term, rcv_home, cmp_home, counts)
    got = lax.all_to_all(pay, AXES, split_axis=0, concat_axis=0, tiled=True)
    fetched = swap(run_pick(got, rcv_filters, cmp_filters))
    even, base, last = run_lags(got, traces, targets, tables)
    settle_pick, energy, rcol, ccol, lines, shots, scale = run_books(
        got, slot_lines, src_line, src_filters)
    send, src_out = run_grad(fetched, (rcol, ccol, shots, tables["d"], even, last, tables["tail"],
                                       tables["i"], base, lines, scale))
    rcv_out, cmp_out = run_settle(swap(send), settle_pick, energy, rcv_filters, cmp_filters)
    return src_out, rcv_out, cmp_out


def solution(mesh):
    rows = P(AXES, None)
    flat = P(AXES)
    return jax.shard_map(
        body,
        mesh=mesh,
        in_specs=(rows, rows, flat, flat, flat, P(), P(), flat, rows, rows, rows),
        out_specs=(rows, rows, rows),
        check_vma=False,
    )
```

time: 83.8 us -> 80.1 us (0.956)
  blocking collectives: 44.7 us -> 20.9 us
  waiting for transfers between devices: 6.93 us -> 26.1 us
  starting transfers between devices: 4.21 us -> 8.03 us
  Pallas kernels: 25.2 us -> 21.7 us
    all_to_all x1 -> x0, blocking collectives: 23.6 us -> none  [body(): lax.all_to_all(send.reshape(DEVS, PAIR, TAPS), AXES, split_axis=0, concat...]
    all_to_all x1 -> x2, waiting for transfers between devices: 6.93 us -> 26.1 us  [swap(): lax.all_to_all(rows.reshape(DEVS, PAIR, TAPS), AXES, split_axis=0, concat...]
    all_to_all x1 -> x2, starting transfers between devices: 4.21 us -> 8.03 us  [swap(): lax.all_to_all(rows.reshape(DEVS, PAIR, TAPS), AXES, split_axis=0, concat...]
    pallas_call x6, Pallas kernels: 25.2 us -> 21.7 us  [the longest x1 9.12 us: run_lags(): pl.pallas_call(lags_kernel, grid=(ROWS // ROWBLK,), out_shape=(hbm(ROWS,...]
  transfers between devices with their start and end apart: 1 -> 2, of which waited for: 1 -> 2; matrix products, arithmetic and copies ran while one was open for 0% -> 1% of each run, Pallas kernels for 15% -> 16%
where the time goes in v3:
time: 80.1 us; the launch traced here: 79.8 us
  waiting for transfers between devices  26.1 us (33%)
  Pallas kernels  21.7 us (27%)
  blocking collectives  20.9 us (26%)
  starting transfers between devices  8.03 us (10%)
  local copies, waits for them, and re-layouts  1.59 us (2%)
  between operations  1.41 us (2%)
    all_to_all x2, waiting for transfers between devices, swap(): lax.all_to_all(rows.reshape(DEVS, PAIR, TAPS), AXES, split_axis=0, concat...  26.1 us
    all_to_all x1, blocking collectives, body(): got = lax.all_to_all(pay, AXES, split_axis=0, concat_axis=0, tiled=True)  20.9 us
    pallas_call x1, Pallas kernels, run_lags(): pl.pallas_call(lags_kernel, grid=(ROWS // ROWBLK,), out_shape=(hbm(ROWS,...  9.12 us
    all_to_all x2, starting transfers between devices, swap(): lax.all_to_all(rows.reshape(DEVS, PAIR, TAPS), AXES, split_axis=0, concat...  8.03 us
    pallas_call x1, Pallas kernels, run_grad(): pl.pallas_call(grad_kernel, out_shape=(vmem(SLOTS, TAPS), vmem(SRC, TAPS)...  4.04 us
    pallas_call x1, Pallas kernels, run_books(): pl.pallas_call(books_kernel, grid=(1,), out_shape=out, in_specs=[whole(a)...  3.29 us
    pallas_call x1, Pallas kernels, run_plan(): pl.pallas_call(plan_kernel, out_shape=(vmem(DEVS, 3 * PAIR), vmem(8, ROWS...  2.53 us
  transfers between devices with their start and end apart: 2, of which 2 were waited for; matrix products, arithmetic and copies ran while one was open for 1% of the time, Pallas kernels for 16%

profile of v3, /device:TPU:1, one launch (start us, length us, event | category | flops | bytes accessed | tf_op | source)
XLA Modules:
  0.0 79.8 jit_solution(11146290021735844805)
XLA Ops:
  0.6 0.0 copy-start.3
  0.6 0.0 copy-start.4
  1.3 2.5 %plan.1 = (f32[128,48]{1,0:T(8,128)S(1)}, f32[8,512]{1,0:T(8,128)S(1)}) custom-call(s32[1]{0:T(128)S(6)} %copy.22.count_ref, s32[1,512]{1,0:T(1,128)} %bitcast.23, s32[1,512]{1,0:T(1,128)} %bitcast.24, s32[128,128]{1,0:T(8,128)} %bitcast.22, s32[256,128]{1,0:T(8,128)} %bitcast.21, bf16[512,2048]{1,0:T(8,128)(2,1)} %traces_ref.1), custom_call_target="tpu_custom_call" | custom-call | tf_op jit(solution)/shard_map/plan/pallas_call | solution.py:352
  3.9 0.0 copy-start.6
  3.9 20.9 %all_to_all.21 = f32[128,1,48]{2,1,0:T(1,128)S(1)} all-to-all(f32[128,1,48]{2,1,0:T(1,128)S(1)} %bitcast.19), channel_id=1, replica_groups=mesh['shot'=32,'line'=4] {'shot','line'}, dimensions={0} | all-to-all | bytes 49152 | tf_op jit(solution)/shard_map/all_to_all | solution.py:441
  24.8 0.0 copy-done.6
  24.8 0.0 copy-start.2
  24.8 0.0 copy-done.3
  24.8 0.0 copy-done.4
  24.8 1.5 %pick.1 = f32[2048,128]{1,0:T(8,128)} custom-call(f32[128,48]{1,0:T(8,128)S(1)} %bitcast.16, f32[128,128]{1,0:T(8,128)S(1)} %copy-done.4, f32[256,128]{1,0:T(8,128)S(1)} %copy-done.3), custom_call_target="tpu_custom_call" | custom-call | tf_op jit(solution)/shard_map/pick/pallas_call | solution.py:366
  26.4 4.2 %all-to-all-start.1 = ((f32[128,16,128]{2,1,0:T(8,128)}), f32[128,16,128]{2,1,0:T(8,128)S(1)}, u32[]{:S(2)}, u32[]{:S(2)}) async-start(f32[128,16,128]{2,1,0:T(8,128)} %bitcast.20), calls=%async_computation.1 | async-start | bytes 2097152 | tf_op jit(solution)/shard_map/all_to_all | solution.py:432
  30.6 0.0 copy-done.2
  30.6 3.3 %books.1 = (bf16[384,2048]{1,0:T(8,128)(2,1)}, f32[384,128]{1,0:T(8,128)}, s16[512,128]{1,0:T(8,128)(2,1)}, s16[512,128]{1,0:T(8,128)(2,1)}, s16[48,512]{1,0:T(8...) custom-call(f32[128,48]{1,0:T(8,128)} %bitcast.17, f32[8,512]{1,0:T(8,128)} %copy-done.6, s32[1,512]{1,0:T(1,128)} %bitcast.25, ...), custom_call_target="tpu_custom_call" | custom-call | tf_op jit(solution)/shard_map/books/pallas_call | solution.py:400
  33.9 9.1 %lags.1 = (f32[512,128]{1,0:T(8,128)}, f32[512,128]{1,0:T(8,128)}, f32[512,256]{1,0:T(8,128)}) custom-call(f32[128,48]{1,0:T(8,128)} %bitcast.18, bf16[512,2048]{1,0:T(8,128)(2,1)} %traces_ref.1, bf16[512,2048]{1,0:T(8,128)(2,1)} %targets_ref.1, bf16[512,256]{1,0:T(8,128)(2,1)} %constant.12.clone.f_ref, bf16[256,256]{1,0:T(8,128)(2,1)} %constant.14.clone.e_ref, ...), custom_call_target="tpu_custom_call" | custom-call | flops 5000000000 | bytes 5000000 | tf_op jit(solution)/shard_map/lags/pallas_call | solution.py:380
  43.0 7.1 %all-to-all-done.1 = f32[128,16,128]{2,1,0:T(8,128)S(1)} async-done(((f32[128,16,128]{2,1,0:T(8,128)}), f32[128,16,128]{2,1,0:T(8,128)S(1)}, u32[]{:S(2)}, u32[]{:S(2)}) %all-to-all-start.1) | async-done | bytes 1048608 | tf_op jit(solution)/shard_map/all_to_all | solution.py:432
  50.1 4.0 %grad.1 = (f32[2048,128]{1,0:T(8,128)S(1)}, f32[4,128]{1,0:T(4,128)S(1)}) custom-call(f32[2048,128]{1,0:T(8,128)S(1)} %bitcast.13, s16[512,128]{1,0:T(8,128)(2,1)} %get-tuple-element.21.refs_0_, s16[512,128]{1,0:T(8,128)(2,1)} %get-tuple-element.22.refs_1_, f32[512,128]{1,0:T(8,128)} %get-tuple-element.23.refs_2_, ...), custom_call_target="tpu_custom_call" | custom-call | tf_op jit(solution)/shard_map/grad/pallas_call | solution.py:411
  54.2 0.0 copy-start.1
  54.2 1.0 %copy-done.1 = f32[2048,128]{1,0:T(8,128)} copy-done((f32[2048,128]{1,0:T(8,128)}, f32[2048,128]{1,0:T(8,128)S(1)}, u32[]{:S(2)}) %copy-start.1) | copy-done | bytes 1048600
  55.1 3.8 %all-to-all-start.2 = ((f32[128,16,128]{2,1,0:T(8,128)}), f32[128,16,128]{2,1,0:T(8,128)S(1)}, u32[]{:S(2)}, u32[]{:S(2)}) async-start(f32[128,16,128]{2,1,0:T(8,128)} %bitcast.15), calls=%async_computation.2 | async-start | bytes 2097152 | tf_op jit(solution)/shard_map/all_to_all | solution.py:432
  59.0 0.6 copy.21
  59.6 19.0 %all-to-all-done.2 = f32[128,16,128]{2,1,0:T(8,128)S(1)} async-done(((f32[128,16,128]{2,1,0:T(8,128)}), f32[128,16,128]{2,1,0:T(8,128)S(1)}, u32[]{:S(2)}, u32[]{:S(2)}) %all-to-all-start.2) | async-done | bytes 1048608 | tf_op jit(solution)/shard_map/all_to_all | solution.py:432
  78.5 0.0 copy-done
  78.5 0.0 copy-done.5
  78.5 1.2 %settle.1 = (f32[128,128]{1,0:T(8,128)}, f32[256,128]{1,0:T(8,128)}) custom-call(f32[2048,128]{1,0:T(8,128)S(1)} %bitcast.14, bf16[384,2048]{1,0:T(8,128)(2,1)S(1)} %copy-done, f32[384,128]{1,0:T(8,128)S(1)} %copy-done.5, f32[128,128]{1,0:T(8,128)S(1)} %copy-done.4, f32[256,128]{1,0:T(8,128)S(1)} %copy-done.3), custom_call_target="tpu_custom_call" | custom-call | tf_op jit(solution)/shard_map/settle/pallas_call | solution.py:422
  (2 shorter events, 0.0 us)
Async XLA Ops:
  0.6 24.2 %copy-start.3 = (f32[256,128]{1,0:T(8,128)S(1)}, f32[256,128]{1,0:T(8,128)}, u32[]{:S(2)}) copy-start(f32[256,128]{1,0:T(8,128)} %cmp_ref.3) | copy-start | bytes 393220
  0.6 24.2 %copy-start.4 = (f32[128,128]{1,0:T(8,128)S(1)}, f32[128,128]{1,0:T(8,128)}, u32[]{:S(2)}) copy-start(f32[128,128]{1,0:T(8,128)} %rcv_ref.3) | copy-start | bytes 196612
  3.9 21.0 %copy-start.6 = (f32[8,512]{1,0:T(8,128)}, f32[8,512]{1,0:T(8,128)S(1)}, u32[]{:S(2)}) copy-start(f32[8,512]{1,0:T(8,128)S(1)} %get-tuple-element.20.slot_ref) | copy-start | bytes 49156
  24.8 5.7 %copy-start.2 = (f32[128,1,48]{2,1,0:T(1,128)}, f32[128,1,48]{2,1,0:T(1,128)S(1)}, u32[]{:S(2)}) copy-start(f32[128,1,48]{2,1,0:T(1,128)S(1)} %all_to_all.21) | copy-start | bytes 73732
  26.4 23.7 %all-to-all-start.1 = ((f32[128,16,128]{2,1,0:T(8,128)}), f32[128,16,128]{2,1,0:T(8,128)S(1)}, u32[]{:S(2)}, u32[]{:S(2)}) async-start(f32[128,16,128]{2,1,0:T(8,128)} %bitcast.20), calls=%async_computation.1 | async-start | bytes 2097152 | tf_op jit(solution)/shard_map/all_to_all | solution.py:432
  50.1 28.4 %copy-start = (bf16[384,2048]{1,0:T(8,128)(2,1)S(1)}, bf16[384,2048]{1,0:T(8,128)(2,1)}, u32[]{:S(2)}) copy-start(bf16[384,2048]{1,0:T(8,128)(2,1)} %get-tuple-element.31.pick_ref) | copy-start | bytes 4718596
  50.1 28.4 %copy-start.5 = (f32[384,128]{1,0:T(8,128)S(1)}, f32[384,128]{1,0:T(8,128)}, u32[]{:S(2)}) copy-start(f32[384,128]{1,0:T(8,128)} %get-tuple-element.32.energy_ref) | copy-start | bytes 589828
  54.2 1.0 %copy-start.1 = (f32[2048,128]{1,0:T(8,128)}, f32[2048,128]{1,0:T(8,128)S(1)}, u32[]{:S(2)}) copy-start(f32[2048,128]{1,0:T(8,128)S(1)} %get-tuple-element.30) | copy-start | bytes 3145732
  55.1 23.4 %all-to-all-start.2 = ((f32[128,16,128]{2,1,0:T(8,128)}), f32[128,16,128]{2,1,0:T(8,128)S(1)}, u32[]{:S(2)}, u32[]{:S(2)}) async-start(f32[128,16,128]{2,1,0:T(8,128)} %bitcast.15), calls=%async_computation.2 | async-start | bytes 2097152 | tf_op jit(solution)/shard_map/all_to_all | solution.py:432

commit v4 on v3

--- a/solution.py
+++ b/solution.py
@@ -20,7 +20,7 @@
 SRC = 4
 WIN = 256
 BLOCKS = NS // TAPS
-ROWBLK = 128
+ROWBLK = 256
 step_size = 0.5
 f32, bf16, i32 = jnp.float32, jnp.bfloat16, jnp.int32
 NT = (((1,), (1,)), ((), ()))
@@ -42,14 +42,12 @@
     lag_phase = np.arange(TAPS)[:, None] * angle[None, :]
     even = 2.0 * np.cos(lag_phase)
     even[0] = 1.0
-    f_high, f_low = split_pair(forward)
     d_pair = np.concatenate(split_pair(forward[:TAPS]), axis=0)
     e_pair = np.concatenate(split_pair(forward[TAPS:]), axis=0)
     i_pair = np.concatenate(split_pair(inverse[:, :TAPS]), axis=1)
     c_pair = np.concatenate(split_pair(even), axis=1)
     tail = split_pair(inverse[:, TAPS:] @ forward[TAPS:])[0]
-    f_pair = np.concatenate([f_high, f_low], axis=0)
-    return dict(f=f_pair, d=d_pair, e=e_pair, i=i_pair, c=c_pair, tail=tail)
+    return dict(d=d_pair, e=e_pair, i=i_pair, c=c_pair, tail=tail)
 
 
 def two(values):
@@ -109,13 +107,12 @@
 
     def look_up(term, home, bits):
         high, low = term >> 7, term & 127
-        halves = jnp.concatenate([jnp.transpose((home >> bits).astype(f32)),
-                                  jnp.transpose((home & (2 ** bits - 1)).astype(f32))], axis=0)
+        halves = jnp.concatenate([home >> bits, home & (2 ** bits - 1)], axis=0)
         rows = home.shape[0]
-        both = mm(halves.astype(bf16), flag16(iota16((rows, ROWS), 0) == row16(high, rows)))
-        pick_low = iota((128, ROWS), 0) == low
-        return (jnp.sum(jnp.where(pick_low, both[:128], 0.0), axis=0, keepdims=True),
-                jnp.sum(jnp.where(pick_low, both[128:], 0.0), axis=0, keepdims=True))
+        both = mm(halves.astype(f32).astype(bf16), flag16(iota16((128, ROWS), 0) == row16(low, 128)))
+        pick_high = iota((rows, ROWS), 0) == high
+        return (jnp.sum(jnp.where(pick_high, both[:rows], 0.0), axis=0, keepdims=True),
+                jnp.sum(jnp.where(pick_high, both[rows:], 0.0), axis=0, keepdims=True))
 
     for copy in copies[:4]:
         copy.wait()
@@ -167,9 +164,9 @@
 
 def pick_kernel(got_ref, rcv_ref, cmp_ref, out_hbm, out_ref, sems):
     pairs = [jnp.concatenate(two(t[...]), axis=1) for t in (rcv_ref, cmp_ref)]
-    half = DEVS // 2
+    half = DEVS // 4
     saves = []
-    for h in range(2):
+    for h in range(4):
         got = got_ref[h * half:(h + 1) * half, :PAIR].astype(i32)
         for side, pair in enumerate(pairs):
             lane = iota((half, pair.shape[0]), 1)
@@ -187,32 +184,28 @@
         save.wait()
 
 
-def lags_kernel(after_ref, traces_ref, targets_ref, f_ref, e_ref, i_ref, c_ref, d_ref,
+def lags_kernel(after_ref, traces_ref, targets_ref, e_ref, i_ref, c_ref,
                 even_ref, base_ref, last_ref):
-    f_high, f_low = f_ref[:WIN, :], f_ref[WIN:, :]
     e_pair = e_ref[...]
-    own = jnp.zeros((ROWBLK, WIN), f32)
-    cross = jnp.zeros((ROWBLK, WIN), f32)
+    sign = 1.0 - 2.0 * (iota((1, TAPS), 1) & 1).astype(f32)
+    own = [jnp.zeros((ROWBLK, TAPS), f32)] * 2
+    cross = [jnp.zeros((ROWBLK, TAPS), f32)] * 2
+    back = None
     for b in range(BLOCKS):
         now = traces_ref[:, b * 128:(b + 1) * 128]
         goal = targets_ref[:, b * 128:(b + 1) * 128]
         u = mm(jnp.concatenate([now, now], axis=1), e_pair)
         v = mm(jnp.concatenate([goal, goal], axis=1), e_pair)
-        if b == 0:
-            x = u
-        else:
-            window = traces_ref[:, (b - 1) * 128:(b + 1) * 128]
-            x = mm(window, f_high) + mm(window, f_low)
-        xr, xi = x[:, :TAPS], x[:, TAPS:]
         ur, ui = u[:, :TAPS], u[:, TAPS:]
         vr, vi = v[:, :TAPS], v[:, TAPS:]
-        own = own + jnp.concatenate([xr * ur + xi * ui, xr * ui - xi * ur], axis=1)
-        cross = cross + jnp.concatenate([xr * vr + xi * vi, xr * vi - xi * vr], axis=1)
+        xr, xi = (ur, ui) if b == 0 else (ur + back[0], ui + back[1])
+        own = [own[0] + (xr * ur + xi * ui), own[1] + (xr * ui - xi * ur)]
+        cross = [cross[0] + (xr * vr + xi * vi), cross[1] + (xr * vi - xi * vr)]
+        back = -sign * ui, sign * ur
     i_pair = i_ref[...]
-    even_ref[...] = fine_mm(fine_mm(own, i_pair), c_ref[...])
-    base_ref[...] = fine_mm(cross, i_pair)
-    final = traces_ref[:, (BLOCKS - 1) * 128:]
-    last_ref[...] = mm(jnp.concatenate([final, final], axis=1), d_ref[...])
+    even_ref[...] = fine_mm(fine_mm(jnp.concatenate(own, axis=1), i_pair), c_ref[...])
+    base_ref[...] = fine_mm(jnp.concatenate(cross, axis=1), i_pair)
+    last_ref[...] = jnp.concatenate(back, axis=1)
 
 
 def books_kernel(got_ref, slot_ref, srcloc_ref, src_ref,
@@ -262,14 +255,16 @@
 
 def grad_kernel(fetched_ref, *refs):
     hbm_refs, (out_ref, src_out_ref) = refs[:11], refs[11:13]
-    vmem_refs, sems = refs[13:24], refs[24]
+    vmem_refs, rows_ref, sems = refs[13:24], refs[24], refs[25]
     copies = fetch(hbm_refs, vmem_refs, sems)
     (rcol_ref, ccol_ref, shot_ref, d_ref, even_ref, last_ref, tail_ref, i_ref, base_ref,
      line_ref, scale_ref) = vmem_refs
     chunk = 512
     chunks = SLOTS // chunk
     lane = iota16((ROWS, 128), 1)
-    first_rows = jnp.concatenate(two(fetched_ref[:chunk, :]), axis=1)
+    for k in range(chunks):
+        part = slice(k * chunk, (k + 1) * chunk)
+        rows_ref[part, :] = jnp.concatenate(two(fetched_ref[part, :]), axis=1)
     for copy in copies[:2]:
         copy.wait()
     rcol, ccol = rcol_ref[...], ccol_ref[...]
@@ -278,11 +273,8 @@
         pick = jnp.concatenate(
             [one_hot16(lane + jnp.int16(k * chunk + j * 128), rcol, ccol) for j in range(chunk // 128)],
             axis=1)
-        if k == 0:
-            both = mm(pick, first_rows)
-        else:
-            rows = jnp.concatenate(two(fetched_ref[k * chunk:(k + 1) * chunk, :]), axis=1)
-            both = both + mm(pick, rows)
+        part = mm(pick, rows_ref[k * chunk:(k + 1) * chunk, :])
+        both = part if k == 0 else both + part
     for copy in copies[2:]:
         copy.wait()
     mixed = (shot_ref[...] + (both[:, :TAPS] + both[:, TAPS:])).astype(bf16)
@@ -308,7 +300,9 @@
                                                   * scale_ref[:8, :])[:SRC]
 
 
-def settle_kernel(grads_ref, pick_ref, energy_ref, rcv_ref, cmp_ref, rcv_out_ref, cmp_out_ref):
+def settle_kernel(grads_ref, pick_ref, energy_ref, rcv_ref, cmp_ref, src_ref,
+                  src_out_ref, rcv_out_ref, cmp_out_ref):
+    src_out_ref[...] = src_ref[...]
     total = jnp.zeros((RCV + CMP, 2 * TAPS), f32)
     width = 512
     for k in range(SLOTS // width):
@@ -367,7 +361,7 @@
         pick_kernel,
         out_shape=hbm(SLOTS, TAPS),
         in_specs=[VM] * 3, out_specs=HB,
-        scratch_shapes=[vmem(SLOTS, TAPS), DMA((2,))],
+        scratch_shapes=[vmem(SLOTS, TAPS), DMA((4,))],
         compiler_params=small,
         name="pick",
     )(got, rcv_filters, cmp_filters)
@@ -382,13 +376,13 @@
         grid=(ROWS // ROWBLK,),
         out_shape=(hbm(ROWS, TAPS), hbm(ROWS, TAPS), hbm(ROWS, WIN)),
         in_specs=[pl.BlockSpec((8, 3 * PAIR), lambda i: (0, 0)), blk(NS), blk(NS)]
-        + [whole(tables[n]) for n in "feicd"],
+        + [whole(tables[n]) for n in "eic"],
         out_specs=(blk(TAPS), blk(TAPS), blk(WIN)),
         compiler_params=large,
         cost_estimate=pl.CostEstimate(flops=5 * 10 ** 9, bytes_accessed=5 * 10 ** 6,
                                       transcendentals=0),
         name="lags",
-    )(*in_hbm(got, traces, targets, *[tables[n] for n in "feicd"]))
+    )(*in_hbm(got, traces, targets, *[tables[n] for n in "eic"]))
 
 
 def run_books(got, slot_lines, src_line, src_filters):
@@ -412,20 +406,21 @@
         grad_kernel,
         out_shape=(vmem(SLOTS, TAPS), vmem(SRC, TAPS)),
         in_specs=[VM] + [HB] * len(held), out_specs=(VM, VM),
-        scratch_shapes=[vmem(*a.shape, dtype=a.dtype) for a in held] + [DMA((len(held),))],
+        scratch_shapes=[vmem(*a.shape, dtype=a.dtype) for a in held]
+        + [vmem(SLOTS, 2 * TAPS, dtype=bf16), DMA((len(held),))],
         compiler_params=small,
         name="grad",
     )(pltpu.with_memory_space_constraint(fetched, pltpu.VMEM), *in_hbm(*held))
 
 
-def run_settle(back, settle_pick, energy, rcv_filters, cmp_filters):
+def run_settle(back, settle_pick, energy, rcv_filters, cmp_filters, src_new):
     return pl.pallas_call(
         settle_kernel,
-        out_shape=(shape(RCV, TAPS), shape(CMP, TAPS)),
-        in_specs=[VM] * 5, out_specs=(VM, VM),
+        out_shape=(shape(SRC, TAPS), shape(RCV, TAPS), shape(CMP, TAPS)),
+        in_specs=[VM] * 6, out_specs=(VM, VM, VM),
         compiler_params=small,
         name="settle",
-    )(back, settle_pick, energy, rcv_filters, cmp_filters)
+    )(back, settle_pick, energy, rcv_filters, cmp_filters, src_new)
 
 
 def swap(rows):
@@ -443,10 +438,9 @@
     even, base, last = run_lags(got, traces, targets, tables)
     settle_pick, energy, rcol, ccol, lines, shots, scale = run_books(
         got, slot_lines, src_line, src_filters)
-    send, src_out = run_grad(fetched, (rcol, ccol, shots, tables["d"], even, last, tables["tail"],
+    send, src_new = run_grad(fetched, (rcol, ccol, shots, tables["d"], even, last, tables["tail"],
                                        tables["i"], base, lines, scale))
-    rcv_out, cmp_out = run_settle(swap(send), settle_pick, energy, rcv_filters, cmp_filters)
-    return src_out, rcv_out, cmp_out
+    return run_settle(swap(send), settle_pick, energy, rcv_filters, cmp_filters, src_new)
 
 
 def solution(mesh):

time: 80.1 us -> 78.7 us (0.983)
  blocking collectives: 20.9 us -> 44 us
  waiting for transfers between devices: 26.1 us -> 9.22 us
  starting transfers between devices: 8.03 us -> 4.21 us
  Pallas kernels: 21.7 us -> 19.5 us
  local copies, waits for them, and re-layouts: 1.59 us -> 0.02 us
    all_to_all x0 -> x1, blocking collectives: none -> 23 us  [swap(): lax.all_to_all(rows.reshape(DEVS, PAIR, TAPS), AXES, split_axis=0, concat...]
    all_to_all x2 -> x1, waiting for transfers between devices: 26.1 us -> 9.22 us  [swap(): lax.all_to_all(rows.reshape(DEVS, PAIR, TAPS), AXES, split_axis=0, concat...]
    all_to_all x2 -> x1, starting transfers between devices: 8.03 us -> 4.21 us  [swap(): lax.all_to_all(rows.reshape(DEVS, PAIR, TAPS), AXES, split_axis=0, concat...]
    pallas_call x1, Pallas kernels: 9.12 us -> 7 us  [run_lags(): pl.pallas_call(lags_kernel, grid=(ROWS // ROWBLK,), out_shape=(hbm(ROWS,...]
    unnamed x15 -> x12, local copies, waits for them, and re-layouts: 1.59 us -> 0.02 us
  transfers between devices with their start and end apart: 2 -> 1, of which waited for: 2 -> 1; matrix products, arithmetic and copies ran while one was open for 1% -> 0% of each run, Pallas kernels for 16% -> 13%
where the time goes in v4:
time: 78.7 us; the launch traced here: 78.4 us
  blocking collectives  44 us (56%)
  Pallas kernels  19.5 us (25%)
  waiting for transfers between devices  9.22 us (12%)
  starting transfers between devices  4.21 us (5%)
  between operations  1.39 us (2%)
    all_to_all x1, blocking collectives, swap(): lax.all_to_all(rows.reshape(DEVS, PAIR, TAPS), AXES, split_axis=0, concat...  23 us
    all_to_all x1, blocking collectives, body(): got = lax.all_to_all(pay, AXES, split_axis=0, concat_axis=0, tiled=True)  20.9 us
    all_to_all x1, waiting for transfers between devices, swap(): lax.all_to_all(rows.reshape(DEVS, PAIR, TAPS), AXES, split_axis=0, concat...  9.22 us
    pallas_call x1, Pallas kernels, run_lags(): pl.pallas_call(lags_kernel, grid=(ROWS // ROWBLK,), out_shape=(hbm(ROWS,...  7 us
    all_to_all x1, starting transfers between devices, swap(): lax.all_to_all(rows.reshape(DEVS, PAIR, TAPS), AXES, split_axis=0, concat...  4.21 us
    pallas_call x1, Pallas kernels, run_grad(): pl.pallas_call(grad_kernel, out_shape=(vmem(SLOTS, TAPS), vmem(SRC, TAPS)...  4.04 us
    pallas_call x1, Pallas kernels, run_books(): pl.pallas_call(books_kernel, grid=(1,), out_shape=out, in_specs=[whole(a)...  3.3 us
    pallas_call x1, Pallas kernels, run_plan(): pl.pallas_call(plan_kernel, out_shape=(vmem(DEVS, 3 * PAIR), vmem(8, ROWS...  2.53 us
  transfers between devices with their start and end apart: 1, of which 1 were waited for; matrix products, arithmetic and copies ran while one was open for 0% of the time, Pallas kernels for 13%

profile of v4, /device:TPU:1, one launch (start us, length us, event | category | flops | bytes accessed | tf_op | source)
XLA Modules:
  0.0 78.4 jit_solution(15757302736123924994)
XLA Ops:
  0.6 0.0 copy-start.2
  0.6 0.0 copy-start.3
  1.3 2.5 %plan.1 = (f32[128,48]{1,0:T(8,128)S(1)}, f32[8,512]{1,0:T(8,128)S(1)}) custom-call(s32[1]{0:T(128)S(6)} %copy.20.count_ref, s32[1,512]{1,0:T(1,128)} %bitcast.23, s32[1,512]{1,0:T(1,128)} %bitcast.24, s32[128,128]{1,0:T(8,128)} %bitcast.22, s32[256,128]{1,0:T(8,128)} %bitcast.21, bf16[512,2048]{1,0:T(8,128)(2,1)} %traces_ref.1), custom_call_target="tpu_custom_call" | custom-call | tf_op jit(solution)/shard_map/plan/pallas_call | solution.py:346
  3.9 0.0 copy-start.5
  3.9 20.9 %all_to_all.21 = f32[128,1,48]{2,1,0:T(1,128)S(1)} all-to-all(f32[128,1,48]{2,1,0:T(1,128)S(1)} %bitcast.19), channel_id=1, replica_groups=mesh['shot'=32,'line'=4] {'shot','line'}, dimensions={0} | all-to-all | bytes 49152 | tf_op jit(solution)/shard_map/all_to_all | solution.py:436
  24.8 0.0 copy-done.5
  24.8 0.0 copy-start.1
  24.8 0.0 copy-done.2
  24.8 0.0 copy-done.3
  24.8 1.4 %pick.1 = f32[2048,128]{1,0:T(8,128)} custom-call(f32[128,48]{1,0:T(8,128)S(1)} %bitcast.16, f32[128,128]{1,0:T(8,128)S(1)} %copy-done.3, f32[256,128]{1,0:T(8,128)S(1)} %copy-done.2), custom_call_target="tpu_custom_call" | custom-call | tf_op jit(solution)/shard_map/pick/pallas_call | solution.py:360
  26.3 4.2 %all-to-all-start.1 = ((f32[128,16,128]{2,1,0:T(8,128)}), f32[128,16,128]{2,1,0:T(8,128)S(1)}, u32[]{:S(2)}, u32[]{:S(2)}) async-start(f32[128,16,128]{2,1,0:T(8,128)} %bitcast.20), calls=%async_computation.1 | async-start | bytes 2097152 | tf_op jit(solution)/shard_map/all_to_all | solution.py:427
  30.5 0.0 copy-done.1
  30.5 3.3 %books.1 = (bf16[384,2048]{1,0:T(8,128)(2,1)}, f32[384,128]{1,0:T(8,128)}, s16[512,128]{1,0:T(8,128)(2,1)}, s16[512,128]{1,0:T(8,128)(2,1)}, s16[48,512]{1,0:T(8...) custom-call(f32[128,48]{1,0:T(8,128)} %bitcast.17, f32[8,512]{1,0:T(8,128)} %copy-done.5, s32[1,512]{1,0:T(1,128)} %bitcast.25, ...), custom_call_target="tpu_custom_call" | custom-call | tf_op jit(solution)/shard_map/books/pallas_call | solution.py:394
  33.8 7.0 %lags.1 = (f32[512,128]{1,0:T(8,128)}, f32[512,128]{1,0:T(8,128)}, f32[512,256]{1,0:T(8,128)}) custom-call(f32[128,48]{1,0:T(8,128)} %bitcast.18, bf16[512,2048]{1,0:T(8,128)(2,1)} %traces_ref.1, bf16[512,2048]{1,0:T(8,128)(2,1)} %targets_ref.1, bf16[256,256]{1,0:T(8,128)(2,1)} %constant.11.clone.e_ref, bf16[256,256]{1,0:T(8,128)(2,1)} %constant.12.clone.i_ref.refs_7_, ...), custom_call_target="tpu_custom_call" | custom-call | flops 5000000000 | bytes 5000000 | tf_op jit(solution)/shard_map/lags/pallas_call | solution.py:374
  40.8 9.2 %all-to-all-done.1 = f32[128,16,128]{2,1,0:T(8,128)S(1)} async-done(((f32[128,16,128]{2,1,0:T(8,128)}), f32[128,16,128]{2,1,0:T(8,128)S(1)}, u32[]{:S(2)}, u32[]{:S(2)}) %all-to-all-start.1) | async-done | bytes 1048608 | tf_op jit(solution)/shard_map/all_to_all | solution.py:427
  50.0 0.0 copy-start
  50.0 0.0 copy-start.4
  50.0 4.0 %grad.1 = (f32[2048,128]{1,0:T(8,128)S(1)}, f32[4,128]{1,0:T(4,128)S(1)}) custom-call(f32[2048,128]{1,0:T(8,128)S(1)} %bitcast.13, s16[512,128]{1,0:T(8,128)(2,1)} %get-tuple-element.19.refs_0_, s16[512,128]{1,0:T(8,128)(2,1)} %get-tuple-element.20.refs_1_, f32[512,128]{1,0:T(8,128)} %get-tuple-element.21.refs_2_, bf16[256,256]{1,0:T(8,128)(2,1)} %constant.10.clone.refs_3_, ...), custom_call_target="tpu_custom_call" | custom-call | tf_op jit(solution)/shard_map/grad/pallas_call | solution.py:405
  54.1 23.0 %all_to_all.22 = f32[128,16,128]{2,1,0:T(8,128)S(1)} all-to-all(f32[128,16,128]{2,1,0:T(8,128)S(1)} %bitcast.15), channel_id=1, replica_groups=mesh['shot'=32,'line'=4] {'shot','line'}, dimensions={0} | all-to-all | bytes 2097152 | tf_op jit(solution)/shard_map/all_to_all | solution.py:427
  77.1 0.0 copy-done
  77.1 0.0 copy-done.4
  77.1 1.3 %settle.1 = (f32[4,128]{1,0:T(4,128)}, f32[128,128]{1,0:T(8,128)}, f32[256,128]{1,0:T(8,128)}) custom-call(f32[2048,128]{1,0:T(8,128)S(1)} %bitcast.14, bf16[384,2048]{1,0:T(8,128)(2,1)S(1)} %copy-done, f32[384,128]{1,0:T(8,128)S(1)} %copy-done.4, f32[128,128]{1,0:T(8,128)S(1)} %copy-done.3, f32[256,128]{1,0:T(8,128)S(1)} %copy-done.2, ...), custom_call_target="tpu_custom_call" | custom-call | tf_op jit(solution)/shard_map/settle/pallas_call | solution.py:417
Async XLA Ops:
  0.6 24.2 %copy-start.2 = (f32[256,128]{1,0:T(8,128)S(1)}, f32[256,128]{1,0:T(8,128)}, u32[]{:S(2)}) copy-start(f32[256,128]{1,0:T(8,128)} %cmp_ref.3) | copy-start | bytes 393220
  0.6 24.2 %copy-start.3 = (f32[128,128]{1,0:T(8,128)S(1)}, f32[128,128]{1,0:T(8,128)}, u32[]{:S(2)}) copy-start(f32[128,128]{1,0:T(8,128)} %rcv_ref.3) | copy-start | bytes 196612
  3.9 21.0 %copy-start.5 = (f32[8,512]{1,0:T(8,128)}, f32[8,512]{1,0:T(8,128)S(1)}, u32[]{:S(2)}) copy-start(f32[8,512]{1,0:T(8,128)S(1)} %get-tuple-element.18.slot_ref) | copy-start | bytes 49156
  24.8 5.7 %copy-start.1 = (f32[128,1,48]{2,1,0:T(1,128)}, f32[128,1,48]{2,1,0:T(1,128)S(1)}, u32[]{:S(2)}) copy-start(f32[128,1,48]{2,1,0:T(1,128)S(1)} %all_to_all.21) | copy-start | bytes 73732
  26.3 23.7 %all-to-all-start.1 = ((f32[128,16,128]{2,1,0:T(8,128)}), f32[128,16,128]{2,1,0:T(8,128)S(1)}, u32[]{:S(2)}, u32[]{:S(2)}) async-start(f32[128,16,128]{2,1,0:T(8,128)} %bitcast.20), calls=%async_computation.1 | async-start | bytes 2097152 | tf_op jit(solution)/shard_map/all_to_all | solution.py:427
  50.0 27.1 %copy-start = (bf16[384,2048]{1,0:T(8,128)(2,1)S(1)}, bf16[384,2048]{1,0:T(8,128)(2,1)}, u32[]{:S(2)}) copy-start(bf16[384,2048]{1,0:T(8,128)(2,1)} %get-tuple-element.28.pick_ref) | copy-start | bytes 4718596
  50.0 27.1 %copy-start.4 = (f32[384,128]{1,0:T(8,128)S(1)}, f32[384,128]{1,0:T(8,128)}, u32[]{:S(2)}) copy-start(f32[384,128]{1,0:T(8,128)} %get-tuple-element.29.energy_ref) | copy-start | bytes 589828

commit v5 on v4

--- a/solution.py
+++ b/solution.py
@@ -212,20 +212,24 @@
                  settle_ref, energy_ref, rcol_ref, ccol_ref, line_ref, shot_ref, scale_ref):
     got = jnp.concatenate([got_ref[...], jnp.zeros((DEVS, 128 - 3 * PAIR), f32)], axis=1)
     turned = jnp.transpose(got)[:3 * PAIR].astype(bf16)
-    q = iota((DEVS, SLOTS), 1)
-    spread = as_bf16((q >> 4) == iota((DEVS, SLOTS), 0))
+    half = DEVS * CAP
+    spread = as_bf16((iota((DEVS, half), 1) >> 3) == iota((DEVS, half), 0))
     wide = mm(turned, spread)
-    line = iota((PAIR, SLOTS), 0)
-    slot = iota((PAIR, SLOTS), 1) & (PAIR - 1)
-    place = jnp.sum(jnp.where(line == slot, wide[:PAIR], 0.0), axis=0, keepdims=True)
-    power = jnp.sum(jnp.where(line == slot, wide[PAIR:2 * PAIR] + wide[2 * PAIR:], 0.0), axis=0, keepdims=True)
-    place = place.astype(i32) + ((iota((1, SLOTS), 1) & CAP) << 4)
-    for c in range(3):
-        rows = iota((128, SLOTS), 0) + c * 128
-        settle_ref[c * 128:(c + 1) * 128, :] = as_bf16(rows == place)
-        energy = jnp.sum(jnp.where(rows == place, power, 0.0), axis=1, keepdims=True)
-        energy_ref[c * 128:(c + 1) * 128, :] = jnp.broadcast_to(
-            step_size / jnp.maximum(energy, 1.0), (128, 128))
+    here = iota((CAP, half), 0) == (iota((CAP, half), 1) & (CAP - 1))
+
+    def line_of(values):
+        return jnp.sum(jnp.where(here, values, 0.0), axis=0, keepdims=True)
+
+    for side, (start, count) in enumerate(((0, RCV), (RCV, CMP))):
+        row = side * CAP
+        place = line_of(wide[row:row + CAP]).astype(i32)
+        power = line_of(wide[PAIR + row:PAIR + row + CAP] + wide[2 * PAIR + row:2 * PAIR + row + CAP])
+        for c in range(count // 128):
+            part = slice(start + c * 128, start + (c + 1) * 128)
+            hit = iota((128, half), 0) + c * 128 == place
+            settle_ref[part, :] = as_bf16(hit)
+            energy = jnp.sum(jnp.where(hit, power, 0.0), axis=1, keepdims=True)
+            energy_ref[part, :] = jnp.broadcast_to(step_size / jnp.maximum(energy, 1.0), (128, 128))
     lines = jnp.concatenate(
         [slot_ref[...], srcloc_ref[...].astype(f32), jnp.zeros((128 - 9, ROWS), f32)], axis=0)
     src = src_ref[...]
@@ -303,14 +307,12 @@
 def settle_kernel(grads_ref, pick_ref, energy_ref, rcv_ref, cmp_ref, src_ref,
                   src_out_ref, rcv_out_ref, cmp_out_ref):
     src_out_ref[...] = src_ref[...]
-    total = jnp.zeros((RCV + CMP, 2 * TAPS), f32)
-    width = 512
-    for k in range(SLOTS // width):
-        rows = jnp.concatenate(two(grads_ref[k * width:(k + 1) * width, :]), axis=1)
-        total = total + mm(pick_ref[:, k * width:(k + 1) * width], rows)
-    change = (total[:, :TAPS] + total[:, TAPS:]) * energy_ref[...]
-    rcv_out_ref[...] = rcv_ref[...] - change[:RCV]
-    cmp_out_ref[...] = cmp_ref[...] - change[RCV:]
+    sides = grads_ref[...].reshape(DEVS, 2, CAP, TAPS)
+    for side, part, table_ref, out_ref in ((0, slice(0, RCV), rcv_ref, rcv_out_ref),
+                                           (1, slice(RCV, RCV + CMP), cmp_ref, cmp_out_ref)):
+        rows = jnp.concatenate(two(sides[:, side].reshape(DEVS * CAP, TAPS)), axis=1)
+        total = mm(pick_ref[part, :], rows)
+        out_ref[...] = table_ref[...] - (total[:, :TAPS] + total[:, TAPS:]) * energy_ref[part, :]
 
 
 def shape(*dims, dtype=f32):
@@ -387,7 +389,7 @@
 
 def run_books(got, slot_lines, src_line, src_filters):
     int16 = jnp.int16
-    out = (hbm(RCV + CMP, SLOTS, dtype=bf16), hbm(RCV + CMP, TAPS),
+    out = (hbm(RCV + CMP, DEVS * CAP, dtype=bf16), hbm(RCV + CMP, TAPS),
            hbm(ROWS, TAPS, dtype=int16), hbm(ROWS, TAPS, dtype=int16),
            hbm(48, ROWS, dtype=int16), hbm(ROWS, TAPS), hbm(16, TAPS))
     args = (got, slot_lines, src_line, src_filters)

time: 78.7 us -> 78.4 us (level)
  Pallas kernels: 19.5 us -> 18.7 us
  transfers between devices with their start and end apart: 1 -> 1, of which waited for: 1 -> 1; matrix products, arithmetic and copies ran while one was open for 0% -> 0% of each run, Pallas kernels for 13% -> 12%
where the time goes in v5:
time: 78.4 us; the launch traced here: 78.1 us
  blocking collectives  44 us (56%)
  Pallas kernels  18.7 us (24%)
  waiting for transfers between devices  9.86 us (13%)
  starting transfers between devices  4.21 us (5%)
  between operations  1.39 us (2%)
    all_to_all x1, blocking collectives, swap(): lax.all_to_all(rows.reshape(DEVS, PAIR, TAPS), AXES, split_axis=0, concat...  23 us
    all_to_all x1, blocking collectives, body(): got = lax.all_to_all(pay, AXES, split_axis=0, concat_axis=0, tiled=True)  20.9 us
    all_to_all x1, waiting for transfers between devices, swap(): lax.all_to_all(rows.reshape(DEVS, PAIR, TAPS), AXES, split_axis=0, concat...  9.86 us
    pallas_call x1, Pallas kernels, run_lags(): pl.pallas_call(lags_kernel, grid=(ROWS // ROWBLK,), out_shape=(hbm(ROWS,...  6.97 us
    all_to_all x1, starting transfers between devices, swap(): lax.all_to_all(rows.reshape(DEVS, PAIR, TAPS), AXES, split_axis=0, concat...  4.21 us
    pallas_call x1, Pallas kernels, run_grad(): pl.pallas_call(grad_kernel, out_shape=(vmem(SLOTS, TAPS), vmem(SRC, TAPS)...  3.99 us
    pallas_call x1, Pallas kernels, run_books(): pl.pallas_call(books_kernel, grid=(1,), out_shape=out, in_specs=[whole(a)...  2.68 us
    pallas_call x1, Pallas kernels, run_plan(): pl.pallas_call(plan_kernel, out_shape=(vmem(DEVS, 3 * PAIR), vmem(8, ROWS...  2.53 us
  transfers between devices with their start and end apart: 1, of which 1 were waited for; matrix products, arithmetic and copies ran while one was open for 0% of the time, Pallas kernels for 12%

profile of v5, /device:TPU:1, one launch (start us, length us, event | category | flops | bytes accessed | tf_op | source)
XLA Modules:
  0.0 78.1 jit_solution(2544501148190748053)
XLA Ops:
  0.6 0.0 copy-start.2
  0.6 0.0 copy-start.3
  1.3 2.5 %plan.1 = (f32[128,48]{1,0:T(8,128)S(1)}, f32[8,512]{1,0:T(8,128)S(1)}) custom-call(s32[1]{0:T(128)S(6)} %copy.20.count_ref, s32[1,512]{1,0:T(1,128)} %bitcast.23, s32[1,512]{1,0:T(1,128)} %bitcast.24, s32[128,128]{1,0:T(8,128)} %bitcast.22, s32[256,128]{1,0:T(8,128)} %bitcast.21, bf16[512,2048]{1,0:T(8,128)(2,1)} %traces_ref.1), custom_call_target="tpu_custom_call" | custom-call | tf_op jit(solution)/shard_map/plan/pallas_call | solution.py:348
  3.9 0.0 copy-start.5
  3.9 20.9 %all_to_all.21 = f32[128,1,48]{2,1,0:T(1,128)S(1)} all-to-all(f32[128,1,48]{2,1,0:T(1,128)S(1)} %bitcast.19), channel_id=1, replica_groups=mesh['shot'=32,'line'=4] {'shot','line'}, dimensions={0} | all-to-all | bytes 49152 | tf_op jit(solution)/shard_map/all_to_all | solution.py:438
  24.8 0.0 copy-done.5
  24.8 0.0 copy-start.1
  24.8 0.0 copy-done.2
  24.8 0.0 copy-done.3
  24.8 1.4 %pick.1 = f32[2048,128]{1,0:T(8,128)} custom-call(f32[128,48]{1,0:T(8,128)S(1)} %bitcast.16, f32[128,128]{1,0:T(8,128)S(1)} %copy-done.3, f32[256,128]{1,0:T(8,128)S(1)} %copy-done.2), custom_call_target="tpu_custom_call" | custom-call | tf_op jit(solution)/shard_map/pick/pallas_call | solution.py:362
  26.3 4.2 %all-to-all-start.1 = ((f32[128,16,128]{2,1,0:T(8,128)}), f32[128,16,128]{2,1,0:T(8,128)S(1)}, u32[]{:S(2)}, u32[]{:S(2)}) async-start(f32[128,16,128]{2,1,0:T(8,128)} %bitcast.20), calls=%async_computation.1 | async-start | bytes 2097152 | tf_op jit(solution)/shard_map/all_to_all | solution.py:429
  30.5 0.0 copy-done.1
  30.5 2.7 %books.1 = (bf16[384,1024]{1,0:T(8,128)(2,1)}, f32[384,128]{1,0:T(8,128)}, s16[512,128]{1,0:T(8,128)(2,1)}, s16[512,128]{1,0:T(8,128)(2,1)}, s16[48,512]{1,0:T(8...) custom-call(f32[128,48]{1,0:T(8,128)} %bitcast.17, f32[8,512]{1,0:T(8,128)} %copy-done.5, s32[1,512]{1,0:T(1,128)} %bitcast.25, ...), custom_call_target="tpu_custom_call" | custom-call | tf_op jit(solution)/shard_map/books/pallas_call | solution.py:396
  33.2 7.0 %lags.1 = (f32[512,128]{1,0:T(8,128)}, f32[512,128]{1,0:T(8,128)}, f32[512,256]{1,0:T(8,128)}) custom-call(f32[128,48]{1,0:T(8,128)} %bitcast.18, bf16[512,2048]{1,0:T(8,128)(2,1)} %traces_ref.1, bf16[512,2048]{1,0:T(8,128)(2,1)} %targets_ref.1, bf16[256,256]{1,0:T(8,128)(2,1)} %constant.11.clone.e_ref, bf16[256,256]{1,0:T(8,128)(2,1)} %constant.12.clone.i_ref.refs_7_, ...), custom_call_target="tpu_custom_call" | custom-call | flops 5000000000 | bytes 5000000 | tf_op jit(solution)/shard_map/lags/pallas_call | solution.py:376
  40.2 9.9 %all-to-all-done.1 = f32[128,16,128]{2,1,0:T(8,128)S(1)} async-done(((f32[128,16,128]{2,1,0:T(8,128)}), f32[128,16,128]{2,1,0:T(8,128)S(1)}, u32[]{:S(2)}, u32[]{:S(2)}) %all-to-all-start.1) | async-done | bytes 1048608 | tf_op jit(solution)/shard_map/all_to_all | solution.py:429
  50.0 0.0 copy-start
  50.0 0.0 copy-start.4
  50.0 4.0 %grad.1 = (f32[2048,128]{1,0:T(8,128)S(1)}, f32[4,128]{1,0:T(4,128)S(1)}) custom-call(f32[2048,128]{1,0:T(8,128)S(1)} %bitcast.13, s16[512,128]{1,0:T(8,128)(2,1)} %get-tuple-element.19.refs_0_, s16[512,128]{1,0:T(8,128)(2,1)} %get-tuple-element.20.refs_1_, f32[512,128]{1,0:T(8,128)} %get-tuple-element.21.refs_2_, bf16[256,256]{1,0:T(8,128)(2,1)} %constant.10.clone.refs_3_, ...), custom_call_target="tpu_custom_call" | custom-call | tf_op jit(solution)/shard_map/grad/pallas_call | solution.py:407
  54.0 23.0 %all_to_all.22 = f32[128,16,128]{2,1,0:T(8,128)S(1)} all-to-all(f32[128,16,128]{2,1,0:T(8,128)S(1)} %bitcast.15), channel_id=1, replica_groups=mesh['shot'=32,'line'=4] {'shot','line'}, dimensions={0} | all-to-all | bytes 2097152 | tf_op jit(solution)/shard_map/all_to_all | solution.py:429
  77.1 0.0 copy-done
  77.1 0.0 copy-done.4
  77.1 1.1 %settle.1 = (f32[4,128]{1,0:T(4,128)}, f32[128,128]{1,0:T(8,128)}, f32[256,128]{1,0:T(8,128)}) custom-call(f32[2048,128]{1,0:T(8,128)S(1)} %bitcast.14, bf16[384,1024]{1,0:T(8,128)(2,1)S(1)} %copy-done, f32[384,128]{1,0:T(8,128)S(1)} %copy-done.4, f32[128,128]{1,0:T(8,128)S(1)} %copy-done.3, f32[256,128]{1,0:T(8,128)S(1)} %copy-done.2, ...), custom_call_target="tpu_custom_call" | custom-call | tf_op jit(solution)/shard_map/settle/pallas_call | solution.py:419
Async XLA Ops:
  0.6 24.2 %copy-start.2 = (f32[256,128]{1,0:T(8,128)S(1)}, f32[256,128]{1,0:T(8,128)}, u32[]{:S(2)}) copy-start(f32[256,128]{1,0:T(8,128)} %cmp_ref.3) | copy-start | bytes 393220
  0.6 24.2 %copy-start.3 = (f32[128,128]{1,0:T(8,128)S(1)}, f32[128,128]{1,0:T(8,128)}, u32[]{:S(2)}) copy-start(f32[128,128]{1,0:T(8,128)} %rcv_ref.3) | copy-start | bytes 196612
  3.9 21.0 %copy-start.5 = (f32[8,512]{1,0:T(8,128)}, f32[8,512]{1,0:T(8,128)S(1)}, u32[]{:S(2)}) copy-start(f32[8,512]{1,0:T(8,128)S(1)} %get-tuple-element.18.slot_ref) | copy-start | bytes 49156
  24.8 5.7 %copy-start.1 = (f32[128,1,48]{2,1,0:T(1,128)}, f32[128,1,48]{2,1,0:T(1,128)S(1)}, u32[]{:S(2)}) copy-start(f32[128,1,48]{2,1,0:T(1,128)S(1)} %all_to_all.21) | copy-start | bytes 73732
  26.3 23.7 %all-to-all-start.1 = ((f32[128,16,128]{2,1,0:T(8,128)}), f32[128,16,128]{2,1,0:T(8,128)S(1)}, u32[]{:S(2)}, u32[]{:S(2)}) async-start(f32[128,16,128]{2,1,0:T(8,128)} %bitcast.20), calls=%async_computation.1 | async-start | bytes 2097152 | tf_op jit(solution)/shard_map/all_to_all | solution.py:429
  50.0 27.0 %copy-start = (bf16[384,1024]{1,0:T(8,128)(2,1)S(1)}, bf16[384,1024]{1,0:T(8,128)(2,1)}, u32[]{:S(2)}) copy-start(bf16[384,1024]{1,0:T(8,128)(2,1)} %get-tuple-element.28.pick_ref) | copy-start | bytes 2359300
  50.0 27.0 %copy-start.4 = (f32[384,128]{1,0:T(8,128)S(1)}, f32[384,128]{1,0:T(8,128)}, u32[]{:S(2)}) copy-start(f32[384,128]{1,0:T(8,128)} %get-tuple-element.29.energy_ref) | copy-start | bytes 589828

commit v6 on v5

--- a/solution.py
+++ b/solution.py
@@ -46,7 +46,7 @@
     e_pair = np.concatenate(split_pair(forward[TAPS:]), axis=0)
     i_pair = np.concatenate(split_pair(inverse[:, :TAPS]), axis=1)
     c_pair = np.concatenate(split_pair(even), axis=1)
-    tail = split_pair(inverse[:, TAPS:] @ forward[TAPS:])[0]
+    tail = np.concatenate(split_pair(inverse[:, TAPS:] @ forward[TAPS:]), axis=1)
     return dict(d=d_pair, e=e_pair, i=i_pair, c=c_pair, tail=tail)
 
 
@@ -286,7 +286,7 @@
     hr, hi = h[:, :TAPS], h[:, TAPS:]
     xr, xi = last_ref[:, :TAPS], last_ref[:, TAPS:]
     past = jnp.concatenate([xr * hr - xi * hi, xr * hi + xi * hr], axis=1)
-    m = mm(past.astype(bf16), tail_ref[...])
+    m = fine_mm(past, tail_ref[...])
     mr, mi = m[:, :TAPS], m[:, TAPS:]
     even = even_ref[...]
     spectrum = jnp.concatenate(
@@ -363,7 +363,7 @@
         pick_kernel,
         out_shape=hbm(SLOTS, TAPS),
         in_specs=[VM] * 3, out_specs=HB,
-        scratch_shapes=[vmem(SLOTS, TAPS), DMA((4,))],
+        scratch_shapes=[vmem(SLOTS + DEVS, TAPS), DMA((4,))],
         compiler_params=small,
         name="pick",
     )(got, rcv_filters, cmp_filters)

time: 78.4 us -> 78.6 us (level)
  no operation moved by 1% of the time
where the time goes in v6:
time: 78.6 us; the launch traced here: 78.3 us
  blocking collectives  44 us (56%)
  Pallas kernels  18.8 us (24%)
  waiting for transfers between devices  9.86 us (13%)
  starting transfers between devices  4.21 us (5%)
  between operations  1.39 us (2%)
    all_to_all x1, blocking collectives, swap(): lax.all_to_all(rows.reshape(DEVS, PAIR, TAPS), AXES, split_axis=0, concat...  23 us
    all_to_all x1, blocking collectives, body(): got = lax.all_to_all(pay, AXES, split_axis=0, concat_axis=0, tiled=True)  20.9 us
    all_to_all x1, waiting for transfers between devices, swap(): lax.all_to_all(rows.reshape(DEVS, PAIR, TAPS), AXES, split_axis=0, concat...  9.86 us
    pallas_call x1, Pallas kernels, run_lags(): pl.pallas_call(lags_kernel, grid=(ROWS // ROWBLK,), out_shape=(hbm(ROWS,...  6.97 us
    all_to_all x1, starting transfers between devices, swap(): lax.all_to_all(rows.reshape(DEVS, PAIR, TAPS), AXES, split_axis=0, concat...  4.21 us
    pallas_call x1, Pallas kernels, run_grad(): pl.pallas_call(grad_kernel, out_shape=(vmem(SLOTS, TAPS), vmem(SRC, TAPS)...  4.14 us
    pallas_call x1, Pallas kernels, run_books(): pl.pallas_call(books_kernel, grid=(1,), out_shape=out, in_specs=[whole(a)...  2.68 us
    pallas_call x1, Pallas kernels, run_plan(): pl.pallas_call(plan_kernel, out_shape=(vmem(DEVS, 3 * PAIR), vmem(8, ROWS...  2.53 us
  transfers between devices with their start and end apart: 1, of which 1 were waited for; matrix products, arithmetic and copies ran while one was open for 0% of the time, Pallas kernels for 12%

profile of v6, /device:TPU:1, one launch (start us, length us, event | category | flops | bytes accessed | tf_op | source)
XLA Modules:
  0.0 78.3 jit_solution(13794257061649597269)
XLA Ops:
  0.6 0.0 copy-start.2
  0.6 0.0 copy-start.3
  1.3 2.5 %plan.1 = (f32[128,48]{1,0:T(8,128)S(1)}, f32[8,512]{1,0:T(8,128)S(1)}) custom-call(s32[1]{0:T(128)S(6)} %copy.20.count_ref, s32[1,512]{1,0:T(1,128)} %bitcast.23, s32[1,512]{1,0:T(1,128)} %bitcast.24, s32[128,128]{1,0:T(8,128)} %bitcast.22, s32[256,128]{1,0:T(8,128)} %bitcast.21, bf16[512,2048]{1,0:T(8,128)(2,1)} %traces_ref.1), custom_call_target="tpu_custom_call" | custom-call | tf_op jit(solution)/shard_map/plan/pallas_call | solution.py:348
  3.9 0.0 copy-start.5
  3.9 20.9 %all_to_all.21 = f32[128,1,48]{2,1,0:T(1,128)S(1)} all-to-all(f32[128,1,48]{2,1,0:T(1,128)S(1)} %bitcast.19), channel_id=1, replica_groups=mesh['shot'=32,'line'=4] {'shot','line'}, dimensions={0} | all-to-all | bytes 49152 | tf_op jit(solution)/shard_map/all_to_all | solution.py:438
  24.8 0.0 copy-done.5
  24.8 0.0 copy-start.1
  24.8 0.0 copy-done.2
  24.8 0.0 copy-done.3
  24.8 1.4 %pick.1 = f32[2048,128]{1,0:T(8,128)} custom-call(f32[128,48]{1,0:T(8,128)S(1)} %bitcast.16, f32[128,128]{1,0:T(8,128)S(1)} %copy-done.3, f32[256,128]{1,0:T(8,128)S(1)} %copy-done.2), custom_call_target="tpu_custom_call" | custom-call | tf_op jit(solution)/shard_map/pick/pallas_call | solution.py:362
  26.3 4.2 %all-to-all-start.1 = ((f32[128,16,128]{2,1,0:T(8,128)}), f32[128,16,128]{2,1,0:T(8,128)S(1)}, u32[]{:S(2)}, u32[]{:S(2)}) async-start(f32[128,16,128]{2,1,0:T(8,128)} %bitcast.20), calls=%async_computation.1 | async-start | bytes 2097152 | tf_op jit(solution)/shard_map/all_to_all | solution.py:429
  30.5 0.0 copy-done.1
  30.5 2.7 %books.1 = (bf16[384,1024]{1,0:T(8,128)(2,1)}, f32[384,128]{1,0:T(8,128)}, s16[512,128]{1,0:T(8,128)(2,1)}, s16[512,128]{1,0:T(8,128)(2,1)}, s16[48,512]{1,0:T(8...) custom-call(f32[128,48]{1,0:T(8,128)} %bitcast.17, f32[8,512]{1,0:T(8,128)} %copy-done.5, s32[1,512]{1,0:T(1,128)} %bitcast.25, ...), custom_call_target="tpu_custom_call" | custom-call | tf_op jit(solution)/shard_map/books/pallas_call | solution.py:396
  33.2 7.0 %lags.1 = (f32[512,128]{1,0:T(8,128)}, f32[512,128]{1,0:T(8,128)}, f32[512,256]{1,0:T(8,128)}) custom-call(f32[128,48]{1,0:T(8,128)} %bitcast.18, bf16[512,2048]{1,0:T(8,128)(2,1)} %traces_ref.1, bf16[512,2048]{1,0:T(8,128)(2,1)} %targets_ref.1, bf16[256,256]{1,0:T(8,128)(2,1)} %constant.11.clone.e_ref, bf16[256,256]{1,0:T(8,128)(2,1)} %constant.12.clone.i_ref.refs_7_, ...), custom_call_target="tpu_custom_call" | custom-call | flops 5000000000 | bytes 5000000 | tf_op jit(solution)/shard_map/lags/pallas_call | solution.py:376
  40.2 9.9 %all-to-all-done.1 = f32[128,16,128]{2,1,0:T(8,128)S(1)} async-done(((f32[128,16,128]{2,1,0:T(8,128)}), f32[128,16,128]{2,1,0:T(8,128)S(1)}, u32[]{:S(2)}, u32[]{:S(2)}) %all-to-all-start.1) | async-done | bytes 1048608 | tf_op jit(solution)/shard_map/all_to_all | solution.py:429
  50.0 0.0 copy-start
  50.0 0.0 copy-start.4
  50.0 4.1 %grad.1 = (f32[2048,128]{1,0:T(8,128)S(1)}, f32[4,128]{1,0:T(4,128)S(1)}) custom-call(f32[2048,128]{1,0:T(8,128)S(1)} %bitcast.13, s16[512,128]{1,0:T(8,128)(2,1)} %get-tuple-element.19.refs_0_, s16[512,128]{1,0:T(8,128)(2,1)} %get-tuple-element.20.refs_1_, f32[512,128]{1,0:T(8,128)} %get-tuple-element.21.refs_2_, bf16[256,256]{1,0:T(8,128)(2,1)} %constant.10.clone.refs_3_, ...), custom_call_target="tpu_custom_call" | custom-call | tf_op jit(solution)/shard_map/grad/pallas_call | solution.py:407
  54.2 23.0 %all_to_all.22 = f32[128,16,128]{2,1,0:T(8,128)S(1)} all-to-all(f32[128,16,128]{2,1,0:T(8,128)S(1)} %bitcast.15), channel_id=1, replica_groups=mesh['shot'=32,'line'=4] {'shot','line'}, dimensions={0} | all-to-all | bytes 2097152 | tf_op jit(solution)/shard_map/all_to_all | solution.py:429
  77.2 0.0 copy-done
  77.2 0.0 copy-done.4
  77.2 1.1 %settle.1 = (f32[4,128]{1,0:T(4,128)}, f32[128,128]{1,0:T(8,128)}, f32[256,128]{1,0:T(8,128)}) custom-call(f32[2048,128]{1,0:T(8,128)S(1)} %bitcast.14, bf16[384,1024]{1,0:T(8,128)(2,1)S(1)} %copy-done, f32[384,128]{1,0:T(8,128)S(1)} %copy-done.4, f32[128,128]{1,0:T(8,128)S(1)} %copy-done.3, f32[256,128]{1,0:T(8,128)S(1)} %copy-done.2, ...), custom_call_target="tpu_custom_call" | custom-call | tf_op jit(solution)/shard_map/settle/pallas_call | solution.py:419
Async XLA Ops:
  0.6 24.2 %copy-start.2 = (f32[256,128]{1,0:T(8,128)S(1)}, f32[256,128]{1,0:T(8,128)}, u32[]{:S(2)}) copy-start(f32[256,128]{1,0:T(8,128)} %cmp_ref.3) | copy-start | bytes 393220
  0.6 24.2 %copy-start.3 = (f32[128,128]{1,0:T(8,128)S(1)}, f32[128,128]{1,0:T(8,128)}, u32[]{:S(2)}) copy-start(f32[128,128]{1,0:T(8,128)} %rcv_ref.3) | copy-start | bytes 196612
  3.9 21.0 %copy-start.5 = (f32[8,512]{1,0:T(8,128)}, f32[8,512]{1,0:T(8,128)S(1)}, u32[]{:S(2)}) copy-start(f32[8,512]{1,0:T(8,128)S(1)} %get-tuple-element.18.slot_ref) | copy-start | bytes 49156
  24.8 5.7 %copy-start.1 = (f32[128,1,48]{2,1,0:T(1,128)}, f32[128,1,48]{2,1,0:T(1,128)S(1)}, u32[]{:S(2)}) copy-start(f32[128,1,48]{2,1,0:T(1,128)S(1)} %all_to_all.21) | copy-start | bytes 73732
  26.3 23.7 %all-to-all-start.1 = ((f32[128,16,128]{2,1,0:T(8,128)}), f32[128,16,128]{2,1,0:T(8,128)S(1)}, u32[]{:S(2)}, u32[]{:S(2)}) async-start(f32[128,16,128]{2,1,0:T(8,128)} %bitcast.20), calls=%async_computation.1 | async-start | bytes 2097152 | tf_op jit(solution)/shard_map/all_to_all | solution.py:429
  50.0 27.2 %copy-start = (bf16[384,1024]{1,0:T(8,128)(2,1)S(1)}, bf16[384,1024]{1,0:T(8,128)(2,1)}, u32[]{:S(2)}) copy-start(bf16[384,1024]{1,0:T(8,128)(2,1)} %get-tuple-element.28.pick_ref) | copy-start | bytes 2359300
  50.0 27.2 %copy-start.4 = (f32[384,128]{1,0:T(8,128)S(1)}, f32[384,128]{1,0:T(8,128)}, u32[]{:S(2)}) copy-start(f32[384,128]{1,0:T(8,128)} %get-tuple-element.29.energy_ref) | copy-start | bytes 589828

commit v7 on v6

--- a/solution.py
+++ b/solution.py
@@ -96,12 +96,12 @@
     return jnp.concatenate([tile] * (count // 16), axis=0)
 
 
-def plan_kernel(count_ref, rterm_hbm, cterm_hbm, rhome_hbm, chome_hbm, traces_hbm, pay_ref, slot_ref,
-                rterm_ref, cterm_ref, rhome_ref, chome_ref, tbuf, sems):
+def plan_kernel(count_hbm, rterm_hbm, cterm_hbm, rhome_hbm, chome_hbm, traces_hbm, pay_ref, slot_ref,
+                count_ref, rterm_ref, cterm_ref, rhome_ref, chome_ref, tbuf, sems):
     parts = [pl.ds(j * 128, 128) for j in range(4)]
     copies = fetch(
-        [rterm_hbm, cterm_hbm, rhome_hbm, chome_hbm] + [traces_hbm.at[p] for p in parts],
-        [rterm_ref, cterm_ref, rhome_ref, chome_ref] + [tbuf.at[p] for p in parts], sems)
+        [rterm_hbm, cterm_hbm, rhome_hbm, chome_hbm, count_hbm] + [traces_hbm.at[p] for p in parts],
+        [rterm_ref, cterm_ref, rhome_ref, chome_ref, count_ref] + [tbuf.at[p] for p in parts], sems)
     earlier = flag16(iota16((128, 128), 0) < iota16((128, 128), 1))
     count_up = jnp.concatenate([earlier, jnp.ones((128, 128), bf16)], axis=1)
 
@@ -114,11 +114,11 @@
         return (jnp.sum(jnp.where(pick_high, both[:rows], 0.0), axis=0, keepdims=True),
                 jnp.sum(jnp.where(pick_high, both[rows:], 0.0), axis=0, keepdims=True))
 
-    for copy in copies[:4]:
+    for copy in copies[:5]:
         copy.wait()
     r_owner, r_place = look_up(rterm_ref[...], rhome_ref[...], 7)
     c_owner, c_place = look_up(cterm_ref[...], chome_ref[...], 8)
-    for copy in copies[4:]:
+    for copy in copies[5:]:
         copy.wait()
     line128 = iota16((DEVS, ROWS), 0)
     mine16 = [flag16(line128 == row16(owner, DEVS)) for owner in (r_owner, c_owner)]
@@ -142,7 +142,7 @@
         powers.append(jnp.sum(jnp.transpose(total), axis=0, keepdims=True))
     rank = jnp.concatenate(ranks, axis=1)
     r_rank, c_rank = rank[0:1], rank[1:2] + CAP
-    live = (iota((1, ROWS), 1) < count_ref[0]).astype(f32)
+    live = (iota((1, ROWS), 1) < count_ref[:, 0:1]).astype(f32)
     power = jnp.concatenate(powers, axis=1) * live
     slot_ref[...] = jnp.concatenate(
         [r_owner * PAIR + r_rank, c_owner * PAIR + c_rank, live, power, jnp.zeros((4, ROWS), f32)],
@@ -164,9 +164,9 @@
 
 def pick_kernel(got_ref, rcv_ref, cmp_ref, out_hbm, out_ref, sems):
     pairs = [jnp.concatenate(two(t[...]), axis=1) for t in (rcv_ref, cmp_ref)]
-    half = DEVS // 4
+    half = DEVS // 8
     saves = []
-    for h in range(4):
+    for h in range(8):
         got = got_ref[h * half:(h + 1) * half, :PAIR].astype(i32)
         for side, pair in enumerate(pairs):
             lane = iota((half, pair.shape[0]), 1)
@@ -348,14 +348,14 @@
     return pl.pallas_call(
         plan_kernel,
         out_shape=(vmem(DEVS, 3 * PAIR), vmem(8, ROWS)),
-        in_specs=[pl.BlockSpec(memory_space=pltpu.SMEM)] + [HB] * 5,
+        in_specs=[HB] * 6,
         out_specs=(VM, VM),
-        scratch_shapes=[vmem(1, ROWS, dtype=i32), vmem(1, ROWS, dtype=i32),
+        scratch_shapes=[vmem(1, 128, dtype=i32), vmem(1, ROWS, dtype=i32), vmem(1, ROWS, dtype=i32),
                         vmem(128, 128, dtype=i32), vmem(256, 128, dtype=i32),
-                        vmem(ROWS, NS, dtype=bf16), DMA((8,))],
+                        vmem(ROWS, NS, dtype=bf16), DMA((9,))],
         compiler_params=small,
         name="plan",
-    )(counts, *args)
+    )(*in_hbm(jnp.pad(counts, (0, 127)).reshape(1, 128)), *args)
 
 
 def run_pick(got, rcv_filters, cmp_filters):
@@ -363,7 +363,7 @@
         pick_kernel,
         out_shape=hbm(SLOTS, TAPS),
         in_specs=[VM] * 3, out_specs=HB,
-        scratch_shapes=[vmem(SLOTS + DEVS, TAPS), DMA((4,))],
+        scratch_shapes=[vmem(SLOTS + DEVS, TAPS), DMA((8,))],
         compiler_params=small,
         name="pick",
     )(got, rcv_filters, cmp_filters)

time: 78.6 us -> 79.1 us (level)
  no operation moved by 1% of the time
where the time goes in v7:
time: 79.1 us; the launch traced here: 78.7 us
  blocking collectives  44 us (56%)
  Pallas kernels  18.8 us (24%)
  waiting for transfers between devices  9.86 us (12%)
  starting transfers between devices  4.22 us (5%)
  between operations  1.39 us (2%)
    all_to_all x1, blocking collectives, swap(): lax.all_to_all(rows.reshape(DEVS, PAIR, TAPS), AXES, split_axis=0, concat...  23 us
    all_to_all x1, blocking collectives, body(): got = lax.all_to_all(pay, AXES, split_axis=0, concat_axis=0, tiled=True)  20.9 us
    all_to_all x1, waiting for transfers between devices, swap(): lax.all_to_all(rows.reshape(DEVS, PAIR, TAPS), AXES, split_axis=0, concat...  9.86 us
    pallas_call x1, Pallas kernels, run_lags(): pl.pallas_call(lags_kernel, grid=(ROWS // ROWBLK,), out_shape=(hbm(ROWS,...  6.97 us
    all_to_all x1, starting transfers between devices, swap(): lax.all_to_all(rows.reshape(DEVS, PAIR, TAPS), AXES, split_axis=0, concat...  4.22 us
    pallas_call x1, Pallas kernels, run_grad(): pl.pallas_call(grad_kernel, out_shape=(vmem(SLOTS, TAPS), vmem(SRC, TAPS)...  4.14 us
    pallas_call x1, Pallas kernels, run_books(): pl.pallas_call(books_kernel, grid=(1,), out_shape=out, in_specs=[whole(a)...  2.68 us
    pallas_call x1, Pallas kernels, run_plan(): pl.pallas_call(plan_kernel, out_shape=(vmem(DEVS, 3 * PAIR), vmem(8, ROWS...  2.54 us
  transfers between devices with their start and end apart: 1, of which 1 were waited for; matrix products, arithmetic and copies ran while one was open for 0% of the time, Pallas kernels for 12%

profile of v7, /device:TPU:1, one launch (start us, length us, event | category | flops | bytes accessed | tf_op | source)
XLA Modules:
  0.0 78.7 jit_solution(7842499991137468701)
XLA Ops:
  0.6 0.0 copy-start.2
  0.6 0.0 copy-start.3
  1.3 0.5 pad_bitcast_fusion.count_hbm
  1.8 2.5 %plan.1 = (f32[128,48]{1,0:T(8,128)S(1)}, f32[8,512]{1,0:T(8,128)S(1)}) custom-call(s32[1,128]{1,0:T(1,128)} %pad_bitcast_fusion.count_hbm, s32[1,512]{1,0:T(1,128)} %bitcast.25, s32[1,512]{1,0:T(1,128)} %bitcast.26, s32[128,128]{1,0:T(8,128)} %bitcast.24, s32[256,128]{1,0:T(8,128)} %bitcast.23, bf16[512,2048]{1,0:T(8,128)(2,1)} %traces_ref.1), custom_call_target="tpu_custom_call" | custom-call | tf_op jit(solution)/shard_map/plan/pallas_call | solution.py:348
  4.4 0.0 copy-start.5
  4.4 20.9 %all_to_all.21 = f32[128,1,48]{2,1,0:T(1,128)S(1)} all-to-all(f32[128,1,48]{2,1,0:T(1,128)S(1)} %bitcast.21), channel_id=1, replica_groups=mesh['shot'=32,'line'=4] {'shot','line'}, dimensions={0} | all-to-all | bytes 49152 | tf_op jit(solution)/shard_map/all_to_all | solution.py:438
  25.4 0.0 copy-done.5
  25.4 0.0 copy-start.1
  25.4 0.0 copy-done.2
  25.4 0.0 copy-done.3
  25.4 1.4 %pick.1 = f32[2048,128]{1,0:T(8,128)} custom-call(f32[128,48]{1,0:T(8,128)S(1)} %bitcast.18, f32[128,128]{1,0:T(8,128)S(1)} %copy-done.3, f32[256,128]{1,0:T(8,128)S(1)} %copy-done.2), custom_call_target="tpu_custom_call" | custom-call | tf_op jit(solution)/shard_map/pick/pallas_call | solution.py:362
  26.8 4.2 %all-to-all-start.1 = ((f32[128,16,128]{2,1,0:T(8,128)}), f32[128,16,128]{2,1,0:T(8,128)S(1)}, u32[]{:S(2)}, u32[]{:S(2)}) async-start(f32[128,16,128]{2,1,0:T(8,128)} %bitcast.22), calls=%async_computation.1 | async-start | bytes 2097152 | tf_op jit(solution)/shard_map/all_to_all | solution.py:429
  31.0 0.0 copy-done.1
  31.0 2.7 %books.1 = (bf16[384,1024]{1,0:T(8,128)(2,1)}, f32[384,128]{1,0:T(8,128)}, s16[512,128]{1,0:T(8,128)(2,1)}, s16[512,128]{1,0:T(8,128)(2,1)}, s16[48,512]{1,0:T(8...) custom-call(f32[128,48]{1,0:T(8,128)} %bitcast.19, f32[8,512]{1,0:T(8,128)} %copy-done.5, s32[1,512]{1,0:T(1,128)} %bitcast.27, ...), custom_call_target="tpu_custom_call" | custom-call | tf_op jit(solution)/shard_map/books/pallas_call | solution.py:396
  33.7 7.0 %lags.1 = (f32[512,128]{1,0:T(8,128)}, f32[512,128]{1,0:T(8,128)}, f32[512,256]{1,0:T(8,128)}) custom-call(f32[128,48]{1,0:T(8,128)} %bitcast.20, bf16[512,2048]{1,0:T(8,128)(2,1)} %traces_ref.1, bf16[512,2048]{1,0:T(8,128)(2,1)} %targets_ref.1, bf16[256,256]{1,0:T(8,128)(2,1)} %constant.13.clone.e_ref, bf16[256,256]{1,0:T(8,128)(2,1)} %constant.14.clone.i_ref.refs_7_, ...), custom_call_target="tpu_custom_call" | custom-call | flops 5000000000 | bytes 5000000 | tf_op jit(solution)/shard_map/lags/pallas_call | solution.py:376
  40.6 9.9 %all-to-all-done.1 = f32[128,16,128]{2,1,0:T(8,128)S(1)} async-done(((f32[128,16,128]{2,1,0:T(8,128)}), f32[128,16,128]{2,1,0:T(8,128)S(1)}, u32[]{:S(2)}, u32[]{:S(2)}) %all-to-all-start.1) | async-done | bytes 1048608 | tf_op jit(solution)/shard_map/all_to_all | solution.py:429
  50.5 0.0 copy-start
  50.5 0.0 copy-start.4
  50.5 4.1 %grad.1 = (f32[2048,128]{1,0:T(8,128)S(1)}, f32[4,128]{1,0:T(4,128)S(1)}) custom-call(f32[2048,128]{1,0:T(8,128)S(1)} %bitcast.15, s16[512,128]{1,0:T(8,128)(2,1)} %get-tuple-element.19.refs_0_, s16[512,128]{1,0:T(8,128)(2,1)} %get-tuple-element.20.refs_1_, f32[512,128]{1,0:T(8,128)} %get-tuple-element.21.refs_2_, bf16[256,256]{1,0:T(8,128)(2,1)} %constant.12.clone.refs_3_, ...), custom_call_target="tpu_custom_call" | custom-call | tf_op jit(solution)/shard_map/grad/pallas_call | solution.py:407
  54.6 23.0 %all_to_all.22 = f32[128,16,128]{2,1,0:T(8,128)S(1)} all-to-all(f32[128,16,128]{2,1,0:T(8,128)S(1)} %bitcast.17), channel_id=1, replica_groups=mesh['shot'=32,'line'=4] {'shot','line'}, dimensions={0} | all-to-all | bytes 2097152 | tf_op jit(solution)/shard_map/all_to_all | solution.py:429
  77.7 0.0 copy-done
  77.7 0.0 copy-done.4
  77.7 1.1 %settle.1 = (f32[4,128]{1,0:T(4,128)}, f32[128,128]{1,0:T(8,128)}, f32[256,128]{1,0:T(8,128)}) custom-call(f32[2048,128]{1,0:T(8,128)S(1)} %bitcast.16, bf16[384,1024]{1,0:T(8,128)(2,1)S(1)} %copy-done, f32[384,128]{1,0:T(8,128)S(1)} %copy-done.4, f32[128,128]{1,0:T(8,128)S(1)} %copy-done.3, f32[256,128]{1,0:T(8,128)S(1)} %copy-done.2, ...), custom_call_target="tpu_custom_call" | custom-call | tf_op jit(solution)/shard_map/settle/pallas_call | solution.py:419
Async XLA Ops:
  0.6 24.7 %copy-start.2 = (f32[256,128]{1,0:T(8,128)S(1)}, f32[256,128]{1,0:T(8,128)}, u32[]{:S(2)}) copy-start(f32[256,128]{1,0:T(8,128)} %cmp_ref.3) | copy-start | bytes 393220
  0.6 24.7 %copy-start.3 = (f32[128,128]{1,0:T(8,128)S(1)}, f32[128,128]{1,0:T(8,128)}, u32[]{:S(2)}) copy-start(f32[128,128]{1,0:T(8,128)} %rcv_ref.3) | copy-start | bytes 196612
  4.4 21.0 %copy-start.5 = (f32[8,512]{1,0:T(8,128)}, f32[8,512]{1,0:T(8,128)S(1)}, u32[]{:S(2)}) copy-start(f32[8,512]{1,0:T(8,128)S(1)} %get-tuple-element.18.slot_ref) | copy-start | bytes 49156
  25.4 5.6 %copy-start.1 = (f32[128,1,48]{2,1,0:T(1,128)}, f32[128,1,48]{2,1,0:T(1,128)S(1)}, u32[]{:S(2)}) copy-start(f32[128,1,48]{2,1,0:T(1,128)S(1)} %all_to_all.21) | copy-start | bytes 73732
  26.8 23.7 %all-to-all-start.1 = ((f32[128,16,128]{2,1,0:T(8,128)}), f32[128,16,128]{2,1,0:T(8,128)S(1)}, u32[]{:S(2)}, u32[]{:S(2)}) async-start(f32[128,16,128]{2,1,0:T(8,128)} %bitcast.22), calls=%async_computation.1 | async-start | bytes 2097152 | tf_op jit(solution)/shard_map/all_to_all | solution.py:429
  50.5 27.2 %copy-start = (bf16[384,1024]{1,0:T(8,128)(2,1)S(1)}, bf16[384,1024]{1,0:T(8,128)(2,1)}, u32[]{:S(2)}) copy-start(bf16[384,1024]{1,0:T(8,128)(2,1)} %get-tuple-element.28.pick_ref) | copy-start | bytes 2359300
  50.5 27.2 %copy-start.4 = (f32[384,128]{1,0:T(8,128)S(1)}, f32[384,128]{1,0:T(8,128)}, u32[]{:S(2)}) copy-start(f32[384,128]{1,0:T(8,128)} %get-tuple-element.29.energy_ref) | copy-start | bytes 589828
